TPU v7x, 512 devices: a whole 4x4x16 slice. The times are simulated.
512 devices in a mesh: row: 16 (over y, x), col: 32 (over z, core).
Axes of the slice: x: 4, y: 4, z: 16, core: 2. Of those that a mesh axis runs over, the one named last changes fastest.
Arguments:
- pattern: int32 [64, 32], P('row', 'col'), may hold values from 0 to 1, as said below
- values: bfloat16 [64, 32, 128, 128], P('row', 'col'), as said below
- branch_sign: int32 [1], replicated, may hold values from 0 to 65535
Outputs:
- purified: float32 [64, 64, 128, 128], P('row', 'col')
- occupation: float32 [], replicated
Inputs may be any that keep to these rules, and one draw needn't show every extreme that they name: Each block row stores exactly one block in each group of 2 block columns; the pattern is symmetric (block (i, j) is stored exactly when block (j, i) is), and every diagonal block is stored. `values`: X is symmetric: block (i, j) equals the transpose of block (j, i). `branch_sign`: an odd code selects the squaring branch, an even one the branch 2 X - X squared.
All inputs are finite; a program needn't handle non-finite values.
Results may differ from a plain program's by a relative error of at most 0.00115.
Values may be sent and summed in bfloat16 or wider, within the bound.
A program may use at most 64 MiB of HBM per device.

v0:
```python
import jax
import jax.numpy as jnp
from jax import lax
from jax.sharding import PartitionSpec as P

BC = 2


def on_device(pattern, values, branch_sign):
    tile_rows = values.shape[0]
    blk_width = values.shape[2]
    row_rank = lax.axis_index("row")
    col_rank = lax.axis_index("col")
    row_ids = jnp.arange(tile_rows, dtype=jnp.int32)
    global_rows = row_rank * tile_rows + row_ids
    odd_sign = branch_sign[0] % 2 == 1
    col_values, col_pattern = (
        lax.all_gather(values, "row", axis=0, tiled=True),
        lax.all_gather(pattern, "row", axis=0, tiled=True),
    )
    panel_blocks = col_values[:, 0]
    panel_spots = col_pattern[:, 0]
    acc_init = jnp.zeros((tile_rows, BC, blk_width, blk_width), jnp.float32)
    col_start = jnp.int32(0)
    part_values = lax.all_gather(values, "col", axis=1, tiled=True)
    part_spots = lax.all_gather(pattern, "col", axis=1, tiled=True)

    def slot_step(slot_id, inner_sum):
        blocks = lax.dynamic_index_in_dim(part_values, slot_id, 1, keepdims=False)
        spot_ids = lax.dynamic_index_in_dim(part_spots, slot_id, 1, keepdims=False)
        inner_ids = (col_start + slot_id) * BC + spot_ids
        partner = jnp.take(panel_blocks, inner_ids, axis=0)
        target = jnp.take(panel_spots, inner_ids, axis=0)
        products = jnp.einsum("iab,ibc->iac", blocks, partner, preferred_element_type=jnp.float32)
        return inner_sum.at[row_ids, target].add(products)

    accumulated = lax.fori_loop(0, part_values.shape[1], slot_step, acc_init)
    own_dense = acc_init.at[row_ids, pattern[:, 0]].set(values[:, 0].astype(jnp.float32))
    purified = jnp.where(odd_sign, accumulated, 2.0 * own_dense - accumulated)
    order_total = tile_rows * lax.axis_size("row") * blk_width
    global_cols = col_rank * BC + jnp.arange(BC, dtype=jnp.int32)
    on_diagonal = global_rows[:, None] == global_cols[None, :]
    block_traces = jnp.trace(purified, axis1=2, axis2=3)
    trace_total = lax.psum(jnp.sum(jnp.where(on_diagonal, block_traces, 0.0)), ("row", "col"))
    return (purified, trace_total / order_total)


def solution(mesh):
    in_specs = (P("row", "col"), P("row", "col", None, None), P())
    out_specs = (P("row", "col", None, None), P())
    return jax.shard_map(
        on_device, mesh=mesh, in_specs=in_specs, out_specs=out_specs, check_vma=False
    )
```

profile of v0, /device:TPU:1, one launch (start us, length us, event | category | flops | bytes accessed | tf_op | source)
XLA Modules:
  0.0 420.5 jit_solution(13929762512996584730)
XLA Ops:
  9.3 37.5 %all-gather = s32[32,1,4]{2,1,0:T(1,128)S(1)} all-gather(s32[1,1,4]{2,1,0:T(1,128)} %bitcast.44), channel_id=1, replica_groups=mesh['row'=16,'col'=32] {'col'}, dimensions={0}, use_global_device_ids=true | all-gather | bytes 528 | tf_op jit(solution)/shard_map/all_gather | solution.py:26
  52.0 12.8 %all-reduce = s32[64]{0:T(128)S(1)} all-reduce(s32[64]{0:T(128)S(1)} %bitcast_dynamic-update-slice_fusion), channel_id=1, replica_groups=mesh['row'=16,'col'=32] {'row'}, use_global_device_ids=true, to_apply=%add | all-reduce | flops 64 | bytes 512 | tf_op jit(solution)/shard_map/squeeze | solution.py:22
  64.8 11.0 %all-gather.6.cloned.1.call-done = bf16[64,1,128,128]{3,2,1,0:T(8,128)(2,1)} async-done(((bf16[4,1,128,128]{3,2,1,0:T(8,128)(2,1)}), bf16[64,1,128,128]{3,2,1,0:T(8,128)(2,1)}) %all-gather.6.cloned.1.call-update) | async-done | bytes 2097168 | tf_op jit(solution)/shard_map/all_gather | solution.py:18
  75.8 76.6 %all-gather.4.cloned.1.call-done = bf16[4,32,128,128]{3,2,0,1:T(8,128)(2,1)} async-done(((bf16[4,1,128,128]{3,2,0,1:T(8,128)(2,1)}), bf16[4,32,128,128]{3,2,0,1:T(8,128)(2,1)}) %all-gather.4.cloned.1.call-update) | async-done | bytes 4194320 | tf_op jit(solution)/shard_map/all_gather | solution.py:25
  152.4 154.6 %while.14 = (s32[]{:T(128)}, f32[4,2,128,128]{3,2,1,0:T(8,128)S(1)}, s32[4,32]{0,1:T(8,128)S(1)}, s32[64]{0:T(128)S(1)}, bf16[4,32,128,128]{3,2,0,1:T(8,128)(2,1...) while((s32[]{:T(128)}, f32[4,2,128,128]{3,2,1,0:T(8,128)S(1)}, ...), condition=%wide.region_2.3_spmd.clone, body=%wide.region_0.2_spmd.clone.sunk | while | flops 16909408 | bytes 1577777 | solution.py:37
  157.3 2.2 gather_fusion.1
  162.1 2.2 gather_fusion.1
  167.0 2.2 gather_fusion.1
  171.8 2.2 gather_fusion.1
  186.3 2.2 gather_fusion.1
  191.1 2.2 gather_fusion.1
  196.0 2.2 gather_fusion.1
  200.8 2.2 gather_fusion.1
  210.4 2.2 gather_fusion.1
  215.3 2.2 gather_fusion.1
  224.9 2.2 gather_fusion.1
  229.8 2.2 gather_fusion.1
  234.6 2.2 gather_fusion.1
  239.4 2.2 gather_fusion.1
  253.9 2.2 gather_fusion.1
  273.3 2.2 gather_fusion.1
  278.1 2.2 gather_fusion.1
  282.9 2.2 gather_fusion.1
  308.6 103.3 %psum.7 = f32[]{:T(128)} all-reduce(f32[]{:T(128)} %select_reduce_fusion.1), channel_id=1, replica_groups=mesh['row'=16,'col'=32] {'row','col'}, use_global_device_ids=true, to_apply=%region_6.7 | all-reduce | flops 1 | bytes 8 | tf_op jit(solution)/shard_map/psum | solution.py:44
  (225 shorter events, 121.5 us)
Async XLA Ops:
  7.2 68.6 %all-gather.6.cloned.1.call-start = ((), (), s32[]{:S(2)}) async-start(), calls=%async_computation.1 | async-start | bytes 2228224 | tf_op jit(solution)/shard_map/all_gather | solution.py:18
  7.9 144.5 %all-gather.4.cloned.1.call-start = ((), (), s32[]{:S(2)}) async-start(), calls=%async_computation | async-start | bytes 4325376 | tf_op jit(solution)/shard_map/all_gather | solution.py:25
Sparse Core Ops, SparseCore 0:
  11.0 64.7 all-gather.5
  77.9 74.4 all-gather.3
where the time goes:
time: 422 us; the launch traced here: 420 us
  blocking collectives  154 us (36%)
  local copies, waits for them, and re-layouts  92.6 us (22%)
  waiting for transfers between devices  88.9 us (21%)
  matrix products  37.1 us (9%)
  other arithmetic  29.3 us (7%)
  between operations  17.2 us (4%)
    psum x1, blocking collectives, on_device(): lax.psum(jnp.sum(jnp.where(on_diagonal, block_traces, 0.0)), ('row', 'col'))  103 us
    all_gather x1, waiting for transfers between devices, on_device(): part_values = lax.all_gather(values, 'col', axis=1, tiled=True)  76.6 us
    gather x32, local copies, waits for them, and re-layouts, slot_step(): partner = jnp.take(panel_blocks, inner_ids, axis=0)  69.2 us
    all_gather x1, blocking collectives, on_device(): part_spots = lax.all_gather(pattern, 'col', axis=1, tiled=True)  37.5 us
    dot_general x32, matrix products, slot_step(): jnp.einsum('iab,ibc->iac', blocks, partner, preferred_element_type=jnp.fl...  37.1 us
    scatter-add x32, other arithmetic, slot_step(): return inner_sum.at[row_ids, target].add(products)  24.9 us
    gather x32, local copies, waits for them, and re-layouts, slot_step(): target = jnp.take(panel_spots, inner_ids, axis=0)  20.5 us
    squeeze x1, blocking collectives, on_device(): panel_spots = col_pattern[:, 0]  12.8 us
  transfers between devices with their start and end apart: 2, of which 2 were waited for; matrix products, arithmetic and copies ran while one was open for 1% of the time, Pallas kernels for 0%

commit v1 on v0

v1 whole, which is shorter than its diff:
```python
import functools

import jax
import jax.numpy as jnp
from jax import lax
from jax.experimental import pallas as pl
from jax.experimental.pallas import tpu as pltpu
from jax.sharding import PartitionSpec as P

MESH = pl.DeviceIdType.MESH
NX, NY, NZ = 4, 4, 16
BLK = 128
ROWS = 4
META = ROWS * BLK
CHUNK = META + 16
SPLIT = 2 * BLK
PIECES = ((0, SPLIT), (SPLIT, CHUNK - SPLIT))
F32 = jnp.float32
BF16 = jnp.bfloat16


def kernel(pat_ref, sign_ref, val_ref, out_ref, occ_ref,
           zbuf, pbuf, lhs, rhs, tot, part, load_sem,
           z_send, z_recv, s_send, s_recv, p_send, p_recv, t_send, t_recv):
    row = lax.axis_index("row")
    col = lax.axis_index("col")
    y, x = row // NX, row % NX
    z, core = col // 2, col % 2
    sgn = 1 - 2 * core

    def at_z(dz):
        return (row, ((z + dz + NZ) % NZ) * 2 + core)

    def at_xy(dx, dy):
        return (((y + dy + NY) % NY) * NX + (x + dx + NX) % NX, col)

    sibling = (row, z * 2 + 1 - core)

    def slot_z(dz):
        return (z + dz + NZ) % NZ

    def slot_xy(dx, dy):
        return ((y + dy + NY) % NY) * NX + (x + dx + NX) % NX

    loads = []
    for n, (lo, ln) in enumerate(((0, SPLIT), (SPLIT, META - SPLIT))):
        src = val_ref.at[pl.ds(lo, ln)]
        loads.append(pltpu.make_async_copy(src, zbuf.at[z, core, pl.ds(lo, ln)], load_sem.at[n]))
        loads.append(pltpu.make_async_copy(src, pbuf.at[row, pl.ds(lo, ln)], load_sem.at[2 + n]))
    for load in loads:
        load.start()

    barrier = pltpu.get_barrier_semaphore()
    greet = [at_z(d) for d in (-1, 1, -2, -3, -4, -8, -12)]
    greet += [at_xy(1, 0), at_xy(-1, 0), at_xy(0, 1), at_xy(0, -1), sibling]
    for peer in greet:
        pl.semaphore_signal(barrier, inc=1, device_id=peer, device_id_type=MESH)

    for load in loads:
        load.wait()

    odd = (sign_ref[0] % 2).astype(F32)
    squares = jnp.zeros((8, BLK), F32)
    diag = jnp.zeros((8, BLK), F32)
    r_ids = lax.broadcasted_iota(jnp.int32, (BLK, BLK), 0)
    c_ids = lax.broadcasted_iota(jnp.int32, (BLK, BLK), 1)
    eye = (r_ids == c_ids).astype(F32)
    for i in range(ROWS):
        blk = zbuf[z, core, pl.ds(i * BLK, BLK), :].astype(F32)
        squares += jnp.sum((blk * blk).reshape(BLK // 8, 8, BLK), axis=0)
        on_diag = (col == row * 2 + i // 2).astype(F32)
        diag += jnp.sum((blk * eye).reshape(BLK // 8, 8, BLK), axis=0) * on_diag
    mine = (2.0 * odd - 1.0) * squares + (2.0 - 2.0 * odd) * diag
    mine = jnp.sum(mine, axis=0, keepdims=True)
    hi = mine.astype(BF16).astype(F32)
    mid = (mine - hi).astype(BF16).astype(F32)
    low = mine - hi - mid
    tile_row = lax.broadcasted_iota(jnp.int32, (16, BLK), 0)
    meta = jnp.zeros((16, BLK), F32)
    for i in range(ROWS):
        meta = jnp.where(tile_row == i, pat_ref[i, 0].astype(F32), meta)
    for i, term in enumerate((hi, mid, low)):
        meta = jnp.where(tile_row == ROWS + i, jnp.broadcast_to(term, (16, BLK)), meta)
    meta = meta.astype(BF16)
    zbuf[z, core, pl.ds(META, 16), :] = meta
    pbuf[row, pl.ds(META, 16), :] = meta

    pl.semaphore_wait(barrier, len(greet))

    sent = []

    def send(src, dst, send_sem, recv_sem, peer):
        copy = pltpu.make_async_remote_copy(
            src_ref=src, dst_ref=dst, send_sem=send_sem, recv_sem=recv_sem,
            device_id=peer, device_id_type=MESH)
        copy.start()
        sent.append(copy)

    def arrived(dst, sem):
        pltpu.make_async_copy(dst, dst, sem).wait()

    def z_ref(dz, who, n):
        lo, ln = PIECES[n]
        return zbuf.at[slot_z(dz), who, pl.ds(lo, ln)]

    def z_send_on(way, step, n):
        dz = -step if way == 0 else step
        src = z_ref(dz, core, n)
        send(src, src, z_send.at[way, step, n], z_recv.at[way, step + 1, n], at_z(1 - 2 * way))

    def s_index(way, step):
        return step if way == 0 else (NZ - step) % NZ

    def to_sibling(way, step, n):
        dz = -step if way == 0 else step
        src = z_ref(dz, core, n)
        k = s_index(way, step)
        send(src, src, s_send.at[k, n], s_recv.at[k, n], sibling)

    def from_sibling(way, step, n):
        dz = -step if way == 0 else step
        arrived(z_ref(dz, 1 - core, n), s_recv.at[s_index(way, step), n])

    def z_step(way, step, n):
        dz = -step if way == 0 else step
        arrived(z_ref(dz, core, n), z_recv.at[way, step, n])
        if step < NZ // 2 - 1 or (step == NZ // 2 - 1 and n == way):
            z_send_on(way, step, n)
        to_sibling(way, step, n)

    def forward(n):
        return sgn if n == 0 else -sgn

    def p_xy(n, a, b):
        f = forward(n)
        return (a * f, b * f) if n == 0 else (b * f, a * f)

    def p_ref(n, a, b):
        lo, ln = PIECES[n]
        return pbuf.at[slot_xy(*p_xy(n, a, b)), pl.ds(lo, ln)]

    AT = {0: 0, -1: 1, 1: 2, 2: 3}

    def p_sem(a, b):
        return AT[a] * 4 + AT[b]

    def p_send_a(n, a, way):
        there = a - way if a - way != -2 else 2
        send(p_ref(n, a, 0), p_ref(n, a, 0), p_send.at[n, p_sem(a, 0), (way + 1) // 2],
             p_recv.at[n, p_sem(there, 0)], at_xy(*p_xy(n, way, 0)))

    def p_send_b(n, a, b, way):
        there = b - way if b - way != -2 else 2
        send(p_ref(n, a, b), p_ref(n, a, b), p_send.at[n, p_sem(a, b), 2 + (way + 1) // 2],
             p_recv.at[n, p_sem(a, there)], at_xy(*p_xy(n, 0, way)))

    def p_arrived(n, a, b):
        arrived(p_ref(n, a, b), p_recv.at[n, p_sem(a, b)])

    def p_first(n, a):
        if a:
            p_arrived(n, a, 0)
        if a == -1:
            p_send_a(n, a, 1)
        p_send_b(n, a, 0, 1)
        p_send_b(n, a, 0, -1)

    def p_second(n, a):
        p_arrived(n, a, -1)
        p_send_b(n, a, -1, 1)

    for n in range(2):
        z_send_on(0, 0, n)
        z_send_on(1, 0, n)
        p_send_a(n, 0, 1)
        p_send_a(n, 0, -1)
    for n in range(2):
        p_first(n, 0)
        to_sibling(0, 0, n)

    def compute(shifts):
        for k, dz in enumerate(shifts):
            slot = slot_z(dz)
            for who in range(2):
                marks = zbuf[slot, who, pl.ds(META, 16), :].astype(F32)
                for i in range(ROWS):
                    spot = jnp.broadcast_to(marks[i:i + 1], (BLK, BLK)).astype(BF16)
                    blk = zbuf[slot, who, pl.ds(i * BLK, BLK), :]
                    at = (k * 2 + who) * 2 * BLK
                    lhs[i * BLK:(i + 1) * BLK, at:at + BLK] = blk * (1 - spot)
                    lhs[i * BLK:(i + 1) * BLK, at + BLK:at + 2 * BLK] = blk * spot
            marks = pbuf[slot, pl.ds(META, 16), :].astype(F32)
            for i in range(ROWS):
                spot = jnp.broadcast_to(marks[i:i + 1], (BLK, BLK)).astype(BF16)
                blk = pbuf[slot, pl.ds(i * BLK, BLK), :]
                at = (k * ROWS + i) * BLK
                rhs[at:at + BLK, :BLK] = blk * (1 - spot)
                rhs[at:at + BLK, BLK:] = blk * spot
        depth = len(shifts) * ROWS * BLK
        prod = jnp.dot(lhs[:, :depth], rhs[:depth, :], preferred_element_type=F32)
        for i in range(ROWS):
            for j in range(2):
                out_ref[i, j] += prod[i * BLK:(i + 1) * BLK, j * BLK:(j + 1) * BLK]

    def z_all(step, n):
        z_step(0, step, n)
        z_step(1, step, n)

    out_ref[...] = jnp.zeros_like(out_ref)

    z_all(1, 0)
    p_first(0, -1)
    p_first(1, -1)
    z_all(1, 1)
    p_first(0, 1)
    p_first(1, 1)

    z_all(2, 0)
    p_first(0, 2)
    p_first(1, 2)
    z_all(2, 1)
    p_second(0, 0)
    p_second(1, 0)

    z_all(3, 0)
    p_second(0, -1)
    p_second(1, -1)
    z_all(3, 1)
    p_second(0, 1)
    p_second(1, 1)

    z_all(4, 0)
    p_second(0, 2)
    p_second(1, 2)
    z_all(4, 1)

    z_all(5, 0)
    for n in range(2):
        for a in (0, -1, 1, 2):
            p_arrived(n, a, 1)
            p_arrived(n, a, 2)

    total = jnp.zeros((1, BLK), F32)
    for slot in range(NX * NY):
        marks = pbuf[slot, pl.ds(META, 16), :].astype(F32)
        total += (marks[ROWS:ROWS + 1] + marks[ROWS + 1:ROWS + 2]) + marks[ROWS + 2:ROWS + 3]

    def put(k, vec):
        tot[k] = jnp.broadcast_to(vec, (8, BLK))

    put(0, total)
    send(tot.at[0], part.at[0], t_send.at[0], t_recv.at[0], sibling)
    z_all(5, 1)

    def ready(step):
        for n in range(2):
            from_sibling(0, step, n)
            if 0 < step < NZ // 2:
                from_sibling(1, step, n)

    ready(0)
    ready(1)
    compute((0,))
    compute((-1, 1))
    arrived(part.at[0], t_recv.at[0])
    total += part[0][:1]
    put(1, total)
    for k in range(3):
        send(tot.at[1], part.at[1 + k], t_send.at[1 + k], t_recv.at[1 + k], at_z(1 + k))
    z_all(6, 0)
    ready(2)
    compute((-2, 2))
    z_all(6, 1)
    ready(3)
    compute((-3, 3))
    for k in range(3):
        arrived(part.at[1 + k], t_recv.at[1 + k])
        total += part[1 + k][:1]
    put(2, total)
    for k in range(3):
        send(tot.at[2], part.at[4 + k], t_send.at[4 + k], t_recv.at[4 + k], at_z((4, 8, 12)[k]))
    z_all(7, 0)
    ready(4)
    compute((-4, 4))
    z_all(7, 1)
    ready(5)
    compute((-5, 5))
    ready(6)
    compute((-6, 6))
    for k in range(3):
        arrived(part.at[4 + k], t_recv.at[4 + k])
        total += part[4 + k][:1]
    occ_ref[...] = jnp.broadcast_to(
        jnp.sum(total, axis=1, keepdims=True) / (NX * NY * ROWS * BLK), occ_ref.shape)
    z_step(0, 8, 0)
    z_step(1, 8, 1)
    ready(7)
    compute((-7, 7))
    ready(8)
    compute((8,))
    for copy in sent:
        copy.wait_send()


def on_device(pattern, values, branch_sign):
    square, occupation = pl.pallas_call(
        kernel,
        out_shape=(
            jax.ShapeDtypeStruct((ROWS, 2, BLK, BLK), F32),
            jax.ShapeDtypeStruct((8, BLK), F32),
        ),
        in_specs=[
            pl.BlockSpec(memory_space=pltpu.SMEM),
            pl.BlockSpec(memory_space=pltpu.SMEM),
            pl.BlockSpec(memory_space=pl.ANY),
        ],
        out_specs=(
            pl.BlockSpec(memory_space=pltpu.VMEM),
            pl.BlockSpec(memory_space=pltpu.VMEM),
        ),
        scratch_shapes=[
            pltpu.VMEM((NZ, 2, CHUNK, BLK), BF16),
            pltpu.VMEM((NX * NY, CHUNK, BLK), BF16),
            pltpu.VMEM((ROWS * BLK, 2 * ROWS * BLK), BF16),
            pltpu.VMEM((2 * ROWS * BLK, 2 * BLK), BF16),
            pltpu.VMEM((3, 8, BLK), F32),
            pltpu.VMEM((7, 8, BLK), F32),
            pltpu.SemaphoreType.DMA((4,)),
            pltpu.SemaphoreType.DMA((2, 8, 2)),
            pltpu.SemaphoreType.DMA((2, 9, 2)),
            pltpu.SemaphoreType.DMA((NZ, 2)),
            pltpu.SemaphoreType.DMA((NZ, 2)),
            pltpu.SemaphoreType.DMA((2, 16, 4)),
            pltpu.SemaphoreType.DMA((2, 16)),
            pltpu.SemaphoreType.DMA((7,)),
            pltpu.SemaphoreType.DMA((7,)),
        ],
        compiler_params=pltpu.CompilerParams(
            collective_id=0, has_side_effects=True, vmem_limit_bytes=32 * 1024 * 1024),
        cost_estimate=pl.CostEstimate(flops=2 * 512 * 8192 * 256, bytes_accessed=1 << 20, transcendentals=0),
    )(pattern, branch_sign, values.reshape(ROWS * BLK, BLK))
    spots = jnp.arange(2, dtype=jnp.int32)
    own = jnp.where((pattern == spots[None, :])[:, :, None, None], values.astype(F32), 0.0)
    odd = branch_sign[0] % 2 == 1
    purified = jnp.where(odd, square, 2.0 * own - square)
    return purified, occupation[0, 0]


def solution(mesh):
    in_specs = (P("row", "col"), P("row", "col", None, None), P())
    out_specs = (P("row", "col", None, None), P())
    return jax.shard_map(
        on_device, mesh=mesh, in_specs=in_specs, out_specs=out_specs, check_vma=False)
```

time: 422 us -> 61.5 us (0.15)
  blocking collectives: 154 us -> 0 us
  local copies, waits for them, and re-layouts: 92.6 us -> 1.26 us
  waiting for transfers between devices: 88.9 us -> 0 us
  Pallas kernels: 0 us -> 56.8 us
  matrix products: 37.1 us -> 0 us
  other arithmetic: 29.3 us -> 2 us
  between operations: 17.2 us -> 1.32 us
    psum x1 -> x0, blocking collectives: 103 us -> none  [on_device(): lax.psum(jnp.sum(jnp.where(on_diagonal, block_traces, 0.0)), ('row', 'col'))]
    gather x64 -> x0, local copies, waits for them, and re-layouts: 89.7 us -> none  [the longest x32 69.2 us: slot_step(): partner = jnp.take(panel_blocks, inner_ids, axis=0)]
    all_gather x2 -> x0, waiting for transfers between devices: 87.6 us -> none  [the longest x1 76.6 us: on_device(): part_values = lax.all_gather(values, 'col', axis=1, tiled=True)]
    pallas_call x0 -> x1, Pallas kernels: none -> 56.8 us  [on_device(): pl.pallas_call(kernel, out_shape=(jax.ShapeDtypeStruct((ROWS, 2, BLK, BLK...]
    all_gather x1 -> x0, blocking collectives: 37.5 us -> none  [on_device(): part_spots = lax.all_gather(pattern, 'col', axis=1, tiled=True)]
    dot_general x32 -> x0, matrix products: 37.1 us -> none  [slot_step(): jnp.einsum('iab,ibc->iac', blocks, partner, preferred_element_type=jnp.fl...]
    scatter-add x32 -> x0, other arithmetic: 24.9 us -> none  [slot_step(): return inner_sum.at[row_ids, target].add(products)]
    squeeze x1 -> x0, blocking collectives: 12.8 us -> none  [on_device(): panel_spots = col_pattern[:, 0]]
  transfers between devices with their start and end apart: 2 -> 0, of which waited for: 2 -> 0; matrix products, arithmetic and copies ran while one was open for 1% -> 0% of each run, Pallas kernels for 0% -> 0%
where the time goes in v1:
time: 61.5 us; the launch traced here: 61.3 us
  Pallas kernels  56.8 us (92%)
  other arithmetic  2 us (3%)
  between operations  1.32 us (2%)
  local copies, waits for them, and re-layouts  1.26 us (2%)
    pallas_call x1, Pallas kernels, on_device(): pl.pallas_call(kernel, out_shape=(jax.ShapeDtypeStruct((ROWS, 2, BLK, BLK...  56.8 us

profile of v1, /device:TPU:1, one launch (start us, length us, event | category | flops | bytes accessed | tf_op | source)
XLA Modules:
  0.0 61.3 jit_solution(5699682207320258546)
XLA Ops:
  1.3 0.0 copy-start.1
  1.3 0.6 %copy-done.1 = s32[4,1]{0,1:T(1,128)S(1)} copy-done((s32[4,1]{0,1:T(1,128)S(1)}, s32[4,1]{0,1:T(1,128)}, u32[]{:S(2)}) %copy-start.1) | copy-done | bytes 40
  1.9 0.1 iota_compare_fusion
  2.0 0.1 copy.5.pat_ref
  2.1 0.0 copy-start
  2.1 1.0 %bitcast_convert_fusion = f32[4,128,128]{2,1,0:T(8,128)S(1)} fusion(bf16[4,1,128,128]{3,2,1,0:T(8,128)(2,1)} %param.4), kind=kLoop, calls=%fused_computation.1 | loop fusion | flops 65536 | bytes 393216 | tf_op jit(solution)/shard_map/jit(_where)/broadcast_in_dim | solution.py:343
  3.1 0.0 copy-done
  3.1 56.8 %shard_map.53 = (f32[4,2,128,128]{3,2,1,0:T(8,128)S(1)}, f32[8,128]{1,0:T(8,128)S(1)}) custom-call(s32[4,1]{1,0:T(4,128)S(1)} %copy.5.pat_ref, s32[1]{0:T(128)} %copy.6.sign_ref, bf16[512,128]{1,0:T(8,128)(2,1)S(1)} %bitcast.10), custom_call_target="tpu_custom_call" | custom-call | flops 2147483648 | bytes 1048576 | tf_op jit(solution)/shard_map/pallas_call | solution.py:306
  59.9 0.5 slice.3
  60.4 0.9 %subtract_select_fusion = f32[4,2,128,128]{3,2,1,0:T(8,128)} fusion(f32[4,2,128,128]{3,2,1,0:T(8,128)S(1)} %get-tuple-element.4, f32[4,128,128]{2,1,0:T(8,128)S(1)} %bitcast_convert_fusion, pred[4,2]{1,0:T(4,128)(4,1)S(1)} %iota_compare_fusion, pred[]{:T(512)S(6)} %eq.22), kind=kLoop, calls=%fused_computation | loop fusion | flops 524288 | bytes 1310729 | tf_op jit(solution)/shard_map/jit(_where)/select_n | solution.py:345
Async XLA Ops:
  1.3 0.7 %copy-start.1 = (s32[4,1]{0,1:T(1,128)S(1)}, s32[4,1]{0,1:T(1,128)}, u32[]{:S(2)}) copy-start(s32[4,1]{0,1:T(1,128)} %param.3) | copy-start | bytes 52
  2.1 1.0 %copy-start = (bf16[4,1,128,128]{3,2,1,0:T(8,128)(2,1)S(1)}, bf16[4,1,128,128]{3,2,1,0:T(8,128)(2,1)}, u32[]{:S(2)}) copy-start(bf16[4,1,128,128]{3,2,1,0:T(8,128)(2,1)} %param.4) | copy-start | bytes 393220

commit v2 on v0

v2 whole, which is shorter than its diff:
```python
import jax
import jax.numpy as jnp
from jax import lax
from jax.experimental import pallas as pl
from jax.experimental.pallas import tpu as pltpu
from jax.sharding import PartitionSpec as P

MESH = pl.DeviceIdType.MESH
NX, NY, NZ = 4, 4, 16
BLK = 128
ROWS = 4
PAIR = 2 * BLK
HALF = PAIR + 16
FAR = NZ // 2
F32 = jnp.float32
BF16 = jnp.bfloat16


def kernel(pat_ref, sign_ref, val_ref, out_ref, occ_ref,
           zbuf, pbuf, lhs, rhs, tot, part, load_sem, own_sem,
           z_send, z_recv, s_send, s_recv, p_send, p_recv, q_send, q_recv, t_send, t_recv):
    row = lax.axis_index("row")
    col = lax.axis_index("col")
    y, x = row // NX, row % NX
    z, core = col // 2, col % 2

    def slot_z(dz):
        return (z + dz + NZ) % NZ

    def slot_xy(dx, dy):
        return ((y + dy + NY) % NY) * NX + (x + dx + NX) % NX

    def at_z(dz, who):
        return (row, slot_z(dz) * 2 + who)

    def at_xy(dx, dy, who):
        return (slot_xy(dx, dy), z * 2 + who)

    sibling = (row, z * 2 + 1 - core)

    loads = [
        pltpu.make_async_copy(
            val_ref.at[pl.ds(n * PAIR, PAIR)], zbuf.at[z, core, n, pl.ds(0, PAIR)], load_sem.at[n])
        for n in range(2)
    ]
    for load in loads:
        load.start()

    barrier = pltpu.get_barrier_semaphore()

    def greet(peers):
        for peer in peers:
            pl.semaphore_signal(barrier, inc=1, device_id=peer, device_id_type=MESH)

    greet([sibling])

    @pl.when(core == 1)
    def _():
        greet([at_z(d, who) for d in (-1, 1) for who in range(2)])

    @pl.when(core == 0)
    def _():
        greet([at_xy(dx, dy, who) for dx, dy in ((1, 0), (-1, 0), (0, 1), (0, -1)) for who in range(2)])
        greet([at_xy(2, 0, 0), at_xy(0, 2, 0)])

    for load in loads:
        load.wait()

    odd = (sign_ref[0] % 2).astype(F32)
    sign = 2.0 * odd - 1.0
    squares = jnp.zeros((8, BLK), F32)
    diag = jnp.zeros((8, BLK), F32)
    eye = (lax.broadcasted_iota(jnp.int32, (BLK, BLK), 0)
           == lax.broadcasted_iota(jnp.int32, (BLK, BLK), 1)).astype(F32)
    tile_row = lax.broadcasted_iota(jnp.int32, (16, BLK), 0)
    for n in range(2):
        meta = jnp.zeros((16, BLK), F32)
        for k in range(2):
            i = 2 * n + k
            spot = pat_ref[0, i].astype(F32)
            meta = jnp.where(tile_row == k, spot, meta)
            blk = zbuf[z, core, n, k * BLK:(k + 1) * BLK, :].astype(F32)
            squares += jnp.sum((blk * blk).reshape(BLK // 8, 8, BLK), axis=0)
            on_diag = (col == row * 2 + n).astype(F32)
            diag += jnp.sum((blk * eye).reshape(BLK // 8, 8, BLK), axis=0) * on_diag
            twice = blk * (2.0 - 2.0 * odd)
            out_ref[i, 0] = twice * (1.0 - spot)
            out_ref[i, 1] = twice * spot
        zbuf[z, core, n, PAIR:, :] = meta.astype(BF16)
    tot[0] = sign * squares + (2.0 - 2.0 * odd) * diag

    @pl.when(core == 0)
    def _():
        pl.semaphore_wait(barrier, 7 + 2)

    @pl.when(core == 1)
    def _():
        pl.semaphore_wait(barrier, 7)

    def send(src, dst, send_sem, recv_sem, peer):
        pltpu.make_async_remote_copy(
            src_ref=src, dst_ref=dst, send_sem=send_sem, recv_sem=recv_sem,
            device_id=peer, device_id_type=MESH).start()

    def done(ref, sem):
        pltpu.make_async_copy(ref, ref, sem).wait()

    piece = zbuf.at[0, 0, 0]
    tile = tot.at[0]

    def z_ref(dz, who, n):
        return zbuf.at[slot_z(dz), who, n]

    def z_shift(way, step):
        return step * (2 * way - 1)

    def z_on(way, step, who, n):
        src = z_ref(z_shift(way, step), who, n)
        send(src, src, z_send.at[way, step, who, n], z_recv.at[way, step + 1, who, n], at_z(1 - 2 * way, 1))

    def z_share(dz, who, n):
        src = z_ref(dz, who, n)
        k = (dz + NZ) % NZ
        send(src, src, s_send.at[k, who, n], s_recv.at[k, who, n], sibling)

    def z_step(step, ways_on):
        for n in range(2):
            for who in range(2):
                for way in range(2):
                    done(piece, z_recv.at[way, step, who, n])
                    if ways_on(way, n):
                        z_on(way, step, who, n)
                    z_share(z_shift(way, step), who, n)

    def p_xy(who, n, a, b):
        f = (1 - 2 * who) * (1 - 2 * n)
        return f * ((1 - n) * a + n * b), f * ((1 - n) * b + n * a)

    def p_ref(who, n, a, b):
        return pbuf.at[who, slot_xy(*p_xy(who, n, a, b)), n]

    def p_at(a):
        return (a + 4) % 4

    def p_first(src, who, n, a, way):
        send(src, p_ref(who, n, a, 0), p_send.at[who, n, p_at(a), 0, (way + 1) // 2],
             p_recv.at[who, n, p_at(a - way), 0], at_xy(*p_xy(who, n, way, 0), 0))

    def p_second(src, who, n, a, b, way):
        send(src, p_ref(who, n, a, b), p_send.at[who, n, p_at(a), p_at(b), 2 + (way + 1) // 2],
             p_recv.at[who, n, p_at(a), p_at(b - way)], at_xy(*p_xy(who, n, 0, way), 0))

    def p_share(who, n, a, b):
        @pl.when(who == 1)
        def _():
            src = p_ref(who, n, a, b)
            send(src, src, q_send.at[n, p_at(a), p_at(b)], q_recv.at[n, p_at(a), p_at(b)], sibling)

    def each(body):
        def step(i, carry):
            body(i // 2, i % 2)
            return carry
        lax.fori_loop(0, 4, step, 0)

    for n in range(2):
        mine = zbuf.at[z, core, n]
        z_on(0, 0, core, n)
        z_on(1, 0, core, n)
        for way in (1, -1):
            p_first(mine, core, n, 0, way)
            p_second(mine, core, n, 0, 0, way)
    for n in range(2):
        z_share(0, core, n)
    own_copies = [
        pltpu.make_async_copy(zbuf.at[z, core, n], pbuf.at[core, row, n], own_sem.at[n]) for n in range(2)]
    for copy in own_copies:
        copy.start()

    def t_copy(k, src, peer):
        send(tot.at[src], part.at[k], t_send.at[k], t_recv.at[k], peer)

    def t_add(src, dst, ks):
        total = tot[src]
        for k in ks:
            done(tile, t_recv.at[k])
            total += part[k]
        tot[dst] = total

    def spread(i):
        return ((i + 1) // 2) * (1 - 2 * (i % 2))

    def compute(i):
        slot = slot_z(spread(i))
        for n in range(2):
            for who in range(2):
                marks = zbuf[slot, who, n, PAIR:, :].astype(F32)
                for k in range(2):
                    spot = jnp.broadcast_to(marks[k:k + 1], (16, BLK)) * sign
                    blk = zbuf[slot, who, n, k * BLK:(k + 1) * BLK, :].reshape(BLK // 16, 16, BLK)
                    r, c = (2 * n + k) * BLK, who * PAIR
                    lhs[r:r + BLK, c:c + BLK] = (blk * (sign - spot).astype(BF16)[None]).reshape(BLK, BLK)
                    lhs[r:r + BLK, c + BLK:c + PAIR] = (blk * spot.astype(BF16)[None]).reshape(BLK, BLK)
            marks = pbuf[core, slot, n, PAIR:, :].astype(F32)
            for k in range(2):
                spot = jnp.broadcast_to(marks[k:k + 1], (16, BLK))
                blk = pbuf[core, slot, n, k * BLK:(k + 1) * BLK, :].reshape(BLK // 16, 16, BLK)
                r = (2 * n + k) * BLK
                rhs[r:r + BLK, :BLK] = (blk * (1.0 - spot).astype(BF16)[None]).reshape(BLK, BLK)
                rhs[r:r + BLK, BLK:] = (blk * spot.astype(BF16)[None]).reshape(BLK, BLK)
        prod = jnp.dot(lhs[...], rhs[...], preferred_element_type=F32)
        for i in range(ROWS):
            for j in range(2):
                out_ref[i, j] += prod[i * BLK:(i + 1) * BLK, j * BLK:(j + 1) * BLK]

    def loop(lo, hi, body):
        def step(i, carry):
            body(i)
            return carry
        lax.fori_loop(lo, hi, step, 0)

    @pl.when(core == 1)
    def _():
        t_copy(0, 0, sibling)
        loop(1, 5, lambda step: z_step(step, lambda way, n: True))
        done(tile, t_recv.at[7])
        tot[1] = part[7]
        for k in range(3):
            t_copy(8 + k, 1, at_z(1 + k, 1))
        z_step(5, lambda way, n: True)
        t_add(1, 2, (8, 9, 10))
        t_copy(11, 2, at_z(4, 1))
        t_copy(12, 2, at_z(-4, 1))
        z_step(6, lambda way, n: True)
        done(tile, t_recv.at[11])
        send(part.at[11], part.at[13], t_send.at[13], t_recv.at[13], at_z(4, 1))

        def p_taken(who, n):
            @pl.when(who == 1)
            def _():
                for a in range(4):
                    for b in range(4):
                        if a or b:
                            done(piece, q_recv.at[n, a, b])
        z_step(7, lambda way, n: way == n)
        each(p_taken)
        for copy in own_copies:
            copy.wait()
        for n in range(2):
            done(piece, s_recv.at[0, 0, n])
        loop(0, 13, compute)
        t_tail = tot[2] + part[11]
        for k in (12, 13):
            done(tile, t_recv.at[k])
            t_tail += part[k]
        tot[3] = t_tail
        tot[4] = t_tail
        t_copy(14, 3, sibling)
        for n in range(2):
            for who in range(2):
                done(piece, z_recv.at[n, FAR, who, n])
                z_share(FAR, who, n)
        loop(13, 16, compute)

    @pl.when(core == 0)
    def _():
        def take(who, n, a, b):
            done(piece, p_recv.at[who, n, p_at(a), p_at(b)])
            p_share(who, n, a, b)

        def first(a):
            def body(who, n):
                done(piece, p_recv.at[who, n, p_at(a), 0])
                src = p_ref(who, n, a, 0)
                if a == -1:
                    p_first(src, who, n, a, 1)
                p_second(src, who, n, a, 0, 1)
                p_second(src, who, n, a, 0, -1)
                p_share(who, n, a, 0)
            each(body)

        def second(a):
            def body(who, n):
                done(piece, p_recv.at[who, n, p_at(a), p_at(-1)])
                p_second(p_ref(who, n, a, -1), who, n, a, -1, 1)
                p_share(who, n, a, -1)
            each(body)

        t_add(0, 1, (0,))
        for k in range(3):
            t_copy(1 + k, 1, at_xy(1 + k, 0, 0))
        first(-1)
        first(1)
        t_add(1, 2, (1, 2, 3))
        for k in range(3):
            t_copy(4 + k, 2, at_xy(0, 1 + k, 0))
        first(2)
        second(0)
        t_add(2, 3, (4, 5, 6))
        t_copy(7, 3, sibling)
        second(-1)
        second(1)
        second(2)
        for b in (1, 2):
            for a in (0, -1, 1, 2):
                each(lambda who, n, a=a, b=b: take(who, n, a, b))
        for copy in own_copies:
            copy.wait()

        def z_taken(i):
            k = (spread(i) + NZ) % NZ
            for n in range(2):
                for who in range(2):
                    done(piece, s_recv.at[k, who, n])
            compute(i)

        for n in range(2):
            done(piece, s_recv.at[0, 1, n])
        compute(0)
        loop(1, 16, z_taken)
        done(tile, t_recv.at[14])
        tot[4] = part[14]

    total = jnp.sum(jnp.sum(tot[4], axis=0, keepdims=True), axis=1, keepdims=True)
    occ_ref[...] = jnp.broadcast_to(total / (NX * NY * ROWS * BLK), occ_ref.shape)

    for n in range(2):
        for way in range(2):
            done(piece, z_send.at[way, 0, core, n])
            done(piece, p_send.at[core, n, 0, 0, way])
            done(piece, p_send.at[core, n, 0, 0, 2 + way])
        done(piece, s_send.at[0, core, n])

    @pl.when(core == 1)
    def _():
        def sent(step):
            for n in range(2):
                for who in range(2):
                    for way in range(2):
                        done(piece, z_send.at[way, step, who, n])
        loop(1, FAR - 1, sent)
        for n in range(2):
            for who in range(2):
                done(piece, z_send.at[n, FAR - 1, who, n])

        def shared(k):
            for n in range(2):
                for who in range(2):
                    done(piece, s_send.at[k, who, n])
        loop(1, NZ, shared)
        for k in (0, 8, 9, 10, 11, 12, 13, 14):
            done(tile, t_send.at[k])

    @pl.when(core == 0)
    def _():
        def sent(who, n):
            done(piece, p_send.at[who, n, 3, 0, 1])
            for a in range(4):
                if a:
                    done(piece, p_send.at[who, n, a, 0, 2])
                    done(piece, p_send.at[who, n, a, 0, 3])
                done(piece, p_send.at[who, n, a, 3, 3])

            @pl.when(who == 1)
            def _():
                for a in range(4):
                    for b in range(4):
                        if a or b:
                            done(piece, q_send.at[n, a, b])
        each(sent)
        for k in (1, 2, 3, 4, 5, 6, 7):
            done(tile, t_send.at[k])


def on_device(pattern, values, branch_sign):
    purified, occupation = pl.pallas_call(
        kernel,
        out_shape=(
            jax.ShapeDtypeStruct((ROWS, 2, BLK, BLK), F32),
            jax.ShapeDtypeStruct((8, BLK), F32),
        ),
        in_specs=[
            pl.BlockSpec(memory_space=pltpu.SMEM),
            pl.BlockSpec(memory_space=pltpu.SMEM),
            pl.BlockSpec(memory_space=pl.ANY),
        ],
        out_specs=(
            pl.BlockSpec(memory_space=pltpu.VMEM),
            pl.BlockSpec(memory_space=pltpu.VMEM),
        ),
        scratch_shapes=[
            pltpu.VMEM((NZ, 2, 2, HALF, BLK), BF16),
            pltpu.VMEM((2, NX * NY, 2, HALF, BLK), BF16),
            pltpu.VMEM((ROWS * BLK, ROWS * BLK), BF16),
            pltpu.VMEM((ROWS * BLK, PAIR), BF16),
            pltpu.VMEM((5, 8, BLK), F32),
            pltpu.VMEM((15, 8, BLK), F32),
            pltpu.SemaphoreType.DMA((2,)),
            pltpu.SemaphoreType.DMA((2,)),
            pltpu.SemaphoreType.DMA((2, FAR, 2, 2)),
            pltpu.SemaphoreType.DMA((2, FAR + 1, 2, 2)),
            pltpu.SemaphoreType.DMA((NZ, 2, 2)),
            pltpu.SemaphoreType.DMA((NZ, 2, 2)),
            pltpu.SemaphoreType.DMA((2, 2, 4, 4, 4)),
            pltpu.SemaphoreType.DMA((2, 2, 4, 4)),
            pltpu.SemaphoreType.DMA((2, 4, 4)),
            pltpu.SemaphoreType.DMA((2, 4, 4)),
            pltpu.SemaphoreType.DMA((15,)),
            pltpu.SemaphoreType.DMA((15,)),
        ],
        compiler_params=pltpu.CompilerParams(
            collective_id=0, has_side_effects=True, vmem_limit_bytes=32 * 1024 * 1024),
        cost_estimate=pl.CostEstimate(flops=2 * 512 * 8192 * 256, bytes_accessed=1 << 20, transcendentals=0),
    )(pattern.reshape(1, ROWS), branch_sign, values.reshape(ROWS * BLK, BLK))
    return purified, occupation[0, 0]


def solution(mesh):
    in_specs = (P("row", "col"), P("row", "col", None, None), P())
    out_specs = (P("row", "col", None, None), P())
    return jax.shard_map(
        on_device, mesh=mesh, in_specs=in_specs, out_specs=out_specs, check_vma=False)
```

time: 422 us -> 55.6 us (0.13)
  blocking collectives: 154 us -> 0 us
  local copies, waits for them, and re-layouts: 92.6 us -> 2.86 us
  waiting for transfers between devices: 88.9 us -> 0 us
  Pallas kernels: 0 us -> 51.3 us
  matrix products: 37.1 us -> 0 us
  other arithmetic: 29.3 us -> 0 us
  between operations: 17.2 us -> 1.29 us
    psum x1 -> x0, blocking collectives: 103 us -> none  [on_device(): lax.psum(jnp.sum(jnp.where(on_diagonal, block_traces, 0.0)), ('row', 'col'))]
    gather x64 -> x0, local copies, waits for them, and re-layouts: 89.7 us -> none  [the longest x32 69.2 us: slot_step(): partner = jnp.take(panel_blocks, inner_ids, axis=0)]
    all_gather x2 -> x0, waiting for transfers between devices: 87.6 us -> none  [the longest x1 76.6 us: on_device(): part_values = lax.all_gather(values, 'col', axis=1, tiled=True)]
    pallas_call x0 -> x1, Pallas kernels: none -> 51.3 us  [on_device(): pl.pallas_call(kernel, out_shape=(jax.ShapeDtypeStruct((ROWS, 2, BLK, BLK...]
    all_gather x1 -> x0, blocking collectives: 37.5 us -> none  [on_device(): part_spots = lax.all_gather(pattern, 'col', axis=1, tiled=True)]
    dot_general x32 -> x0, matrix products: 37.1 us -> none  [slot_step(): jnp.einsum('iab,ibc->iac', blocks, partner, preferred_element_type=jnp.fl...]
    scatter-add x32 -> x0, other arithmetic: 24.9 us -> none  [slot_step(): return inner_sum.at[row_ids, target].add(products)]
    squeeze x1 -> x0, blocking collectives: 12.8 us -> none  [on_device(): panel_spots = col_pattern[:, 0]]
  transfers between devices with their start and end apart: 2 -> 0, of which waited for: 2 -> 0; matrix products, arithmetic and copies ran while one was open for 1% -> 0% of each run, Pallas kernels for 0% -> 0%
where the time goes in v2:
time: 55.6 us; the launch traced here: 55.4 us
  Pallas kernels  51.3 us (92%)
  local copies, waits for them, and re-layouts  2.86 us (5%)
  between operations  1.29 us (2%)
    pallas_call x1, Pallas kernels, on_device(): pl.pallas_call(kernel, out_shape=(jax.ShapeDtypeStruct((ROWS, 2, BLK, BLK...  51.3 us
    unnamed x5, local copies, waits for them, and re-layouts  2.34 us

profile of v2, /device:TPU:1, one launch (start us, length us, event | category | flops | bytes accessed | tf_op | source)
XLA Modules:
  0.0 55.4 jit_solution(6044975801613642411)
XLA Ops:
  1.3 0.0 copy-start.1
  1.3 0.6 %copy-done.1 = s32[4,1]{0,1:T(1,128)S(1)} copy-done((s32[4,1]{0,1:T(1,128)S(1)}, s32[4,1]{0,1:T(1,128)}, u32[]{:S(2)}) %copy-start.1) | copy-done | bytes 40
  1.9 0.0 copy-start
  1.9 0.9 %copy-done = bf16[4,1,128,128]{3,2,1,0:T(8,128)(2,1)S(1)} copy-done((bf16[4,1,128,128]{3,2,1,0:T(8,128)(2,1)S(1)}, bf16[4,1,128,128]{3,2,1,0:T(8,128)(2,1)}, u32[]{:S(2)}) %copy-start) | copy-done | bytes 131096
  2.8 51.3 %shard_map.50 = (f32[4,2,128,128]{3,2,1,0:T(8,128)S(1)}, f32[8,128]{1,0:T(8,128)S(1)}) custom-call(s32[1,4]{1,0:T(1,128)S(1)} %bitcast.4, s32[1]{0:T(128)S(6)} %copy.6.sign_ref, bf16[512,128]{1,0:T(8,128)(2,1)S(1)} %bitcast.3), custom_call_target="tpu_custom_call" | custom-call | flops 2147483648 | bytes 1048576 | tf_op jit(solution)/shard_map/pallas_call | solution.py:375
  54.1 0.5 slice.3
  54.7 0.8 %copy.7 = f32[4,2,128,128]{3,2,1,0:T(8,128)} copy(f32[4,2,128,128]{3,2,1,0:T(8,128)S(1)} %get-tuple-element.8) | data formatting | bytes 1048576
Async XLA Ops:
  1.3 0.7 %copy-start.1 = (s32[4,1]{0,1:T(1,128)S(1)}, s32[4,1]{0,1:T(1,128)}, u32[]{:S(2)}) copy-start(s32[4,1]{0,1:T(1,128)} %param.3) | copy-start | bytes 52
  1.9 0.9 %copy-start = (bf16[4,1,128,128]{3,2,1,0:T(8,128)(2,1)S(1)}, bf16[4,1,128,128]{3,2,1,0:T(8,128)(2,1)}, u32[]{:S(2)}) copy-start(bf16[4,1,128,128]{3,2,1,0:T(8,128)(2,1)} %param.4) | copy-start | bytes 393220

commit v3 on v2

v3 whole, which is shorter than its diff:
```python
import jax
import jax.numpy as jnp
from jax import lax
from jax.experimental import pallas as pl
from jax.experimental.pallas import tpu as pltpu
from jax.sharding import PartitionSpec as P

MESH = pl.DeviceIdType.MESH
NX, NY, NZ = 4, 4, 16
BLK = 128
ROWS = 4
PAIR = 2 * BLK
HALF = PAIR + 16
FAR = NZ // 2
F32 = jnp.float32
BF16 = jnp.bfloat16


def kernel(pat_hbm, sign_ref, val_ref, out_ref, occ_ref,
           zbuf, pbuf, lhs, rhs, tot, part, pat_ref, load_sem, small_sem, own_sem,
           z_send, z_recv, s_send, s_recv, p_send, p_recv, q_send, q_recv, t_send, t_recv):
    row = lax.axis_index("row")
    col = lax.axis_index("col")
    y, x = row // NX, row % NX
    z, core = col // 2, col % 2

    def slot_z(dz):
        return (z + dz + NZ) % NZ

    def slot_xy(dx, dy):
        return ((y + dy + NY) % NY) * NX + (x + dx + NX) % NX

    def at_z(dz, who):
        return (row, slot_z(dz) * 2 + who)

    def at_xy(dx, dy, who):
        return (slot_xy(dx, dy), z * 2 + who)

    sibling = (row, z * 2 + 1 - core)

    barrier = pltpu.get_barrier_semaphore()

    def greet(peers):
        for peer in peers:
            pl.semaphore_signal(barrier, inc=1, device_id=peer, device_id_type=MESH)

    @pl.when(core == 1)
    def _():
        greet([at_z(-1, 1), at_z(1, 1)])

    greet([sibling])

    @pl.when(core == 0)
    def _():
        greet([at_xy(1, 0, 0), at_xy(-1, 0, 0), at_xy(0, 1, 0), at_xy(0, -1, 0), at_xy(2, 0, 0), at_xy(0, 2, 0)])

    small = pltpu.make_async_copy(pat_hbm, pat_ref, small_sem.at[0])
    small.start()
    loads = [
        pltpu.make_async_copy(
            val_ref.at[pl.ds(n * PAIR, PAIR)], zbuf.at[z, core, n, pl.ds(0, PAIR)], load_sem.at[n])
        for n in range(2)
    ]
    for load in loads:
        load.start()

    small.wait()
    odd = (sign_ref[0] % 2).astype(F32)
    sign = 2.0 * odd - 1.0
    spots = [pat_ref[0, i].astype(F32) for i in range(ROWS)]
    tile_row = lax.broadcasted_iota(jnp.int32, (16, BLK), 0)
    for n in range(2):
        marks = jnp.where(tile_row == 0, spots[2 * n], jnp.where(tile_row == 1, spots[2 * n + 1], 0.0))
        zbuf[z, core, n, PAIR:, :] = marks.astype(BF16)
    for load in loads:
        load.wait()

    @pl.when(core == 0)
    def _():
        pl.semaphore_wait(barrier, 7)

    @pl.when(core == 1)
    def _():
        pl.semaphore_wait(barrier, 3)

    def send(src, dst, send_sem, recv_sem, peer):
        pltpu.make_async_remote_copy(
            src_ref=src, dst_ref=dst, send_sem=send_sem, recv_sem=recv_sem,
            device_id=peer, device_id_type=MESH).start()

    def done(ref, sem):
        pltpu.make_async_copy(ref, ref, sem).wait()

    piece = zbuf.at[0, 0, 0]
    tile = tot.at[0]

    def z_ref(dz, who, n):
        return zbuf.at[slot_z(dz), who, n]

    def z_shift(way, step):
        return step * (2 * way - 1)

    def z_on(way, step, who, n):
        dst = z_ref(z_shift(way, step), who, n)
        send(dst, dst, z_send.at[way, step, who, n], z_recv.at[way, step + 1, who, n], at_z(1 - 2 * way, 1))

    def z_share(dz, who, n):
        dst = z_ref(dz, who, n)
        k = (dz + NZ) % NZ
        send(dst, dst, s_send.at[k, who, n], s_recv.at[k, who, n], sibling)

    def z_step(who, step, on=lambda way, n: True):
        for n in range(2):
            for way in range(2):
                done(piece, z_recv.at[way, step, who, n])
                if on(way, n):
                    z_on(way, step, who, n)
                z_share(z_shift(way, step), who, n)

    def z_last(who):
        for n in range(2):
            done(piece, z_recv.at[n, FAR, who, n])
            z_share(FAR, who, n)

    def last_hop(way, n):
        return way == n

    def z_sent(who, step):
        for n in range(2):
            for way in range(2):
                done(piece, z_send.at[way, step, who, n])

    def s_sent(who, step):
        for n in range(2):
            done(piece, s_send.at[NZ - step, who, n])
            done(piece, s_send.at[step, who, n])

    def p_xy(who, n, a, b):
        f = (1 - 2 * who) * (1 - 2 * n)
        return f * ((1 - n) * a + n * b), f * ((1 - n) * b + n * a)

    def p_ref(who, n, a, b):
        return pbuf.at[who, slot_xy(*p_xy(who, n, a, b)), n]

    def p_at(a):
        return (a + 4) % 4

    def p_first(src, who, n, a, way):
        send(src, p_ref(who, n, a, 0), p_send.at[who, n, p_at(a), 0, (way + 1) // 2],
             p_recv.at[who, n, p_at(a - way), 0], at_xy(*p_xy(who, n, way, 0), 0))

    def p_second(src, who, n, a, b, way):
        send(src, p_ref(who, n, a, b), p_send.at[who, n, p_at(a), p_at(b), 2 + (way + 1) // 2],
             p_recv.at[who, n, p_at(a), p_at(b - way)], at_xy(*p_xy(who, n, 0, way), 0))

    def p_share(who, n, a, b):
        @pl.when(who == 1)
        def _():
            src = p_ref(who, n, a, b)
            send(src, src, q_send.at[n, p_at(a), p_at(b)], q_recv.at[n, p_at(a), p_at(b)], sibling)

    def each(body):
        def step(i, carry):
            body(i // 2, i % 2)
            return carry
        lax.fori_loop(0, 4, step, 0)

    @pl.when(core == 1)
    def _():
        for n in range(2):
            z_on(0, 0, 1, n)
            z_on(1, 0, 1, n)

    for n in range(2):
        z_share(0, core, n)
    own_copies = [
        pltpu.make_async_copy(zbuf.at[z, core, n], pbuf.at[core, row, n], own_sem.at[n]) for n in range(2)]
    for copy in own_copies:
        copy.start()

    def own_part():
        squares = jnp.zeros((8, BLK), F32)
        diag = jnp.zeros((8, BLK), F32)
        eye = (lax.broadcasted_iota(jnp.int32, (BLK, BLK), 0)
               == lax.broadcasted_iota(jnp.int32, (BLK, BLK), 1)).astype(F32)
        for i in range(ROWS):
            n, k = i // 2, i % 2
            blk = zbuf[z, core, n, k * BLK:(k + 1) * BLK, :].astype(F32)
            squares += jnp.sum((blk * blk).reshape(BLK // 8, 8, BLK), axis=0)
            on_diag = (col == row * 2 + n).astype(F32)
            diag += jnp.sum((blk * eye).reshape(BLK // 8, 8, BLK), axis=0) * on_diag
            twice = blk * (2.0 - 2.0 * odd)
            out_ref[i, 0] = twice * (1.0 - spots[i])
            out_ref[i, 1] = twice * spots[i]
        tot[0] = sign * squares + (2.0 - 2.0 * odd) * diag

    def t_copy(k, src, peer):
        send(tot.at[src], part.at[k], t_send.at[k], t_recv.at[k], peer)

    def t_add(src, dst, ks):
        total = tot[src]
        for k in ks:
            done(tile, t_recv.at[k])
            total += part[k]
        tot[dst] = total

    def spread(i):
        return ((i + 1) // 2) * (1 - 2 * (i % 2))

    def compute(i, count):
        for g in range(count):
            slot = slot_z(spread(i + g))
            for n in range(2):
                for who in range(2):
                    marks = zbuf[slot, who, n, PAIR:, :].astype(F32)
                    for k in range(2):
                        spot = jnp.broadcast_to(marks[k:k + 1], (16, BLK)) * sign
                        blk = zbuf[slot, who, n, k * BLK:(k + 1) * BLK, :].reshape(BLK // 16, 16, BLK)
                        r, c = (2 * n + k) * BLK, (2 * g + who) * PAIR
                        lhs[r:r + BLK, c:c + BLK] = (blk * (sign - spot).astype(BF16)[None]).reshape(BLK, BLK)
                        lhs[r:r + BLK, c + BLK:c + PAIR] = (blk * spot.astype(BF16)[None]).reshape(BLK, BLK)
                marks = pbuf[core, slot, n, PAIR:, :].astype(F32)
                for k in range(2):
                    spot = jnp.broadcast_to(marks[k:k + 1], (16, BLK))
                    blk = pbuf[core, slot, n, k * BLK:(k + 1) * BLK, :].reshape(BLK // 16, 16, BLK)
                    r = (ROWS * g + 2 * n + k) * BLK
                    rhs[r:r + BLK, :BLK] = (blk * (1.0 - spot).astype(BF16)[None]).reshape(BLK, BLK)
                    rhs[r:r + BLK, BLK:] = (blk * spot.astype(BF16)[None]).reshape(BLK, BLK)
        depth = count * ROWS * BLK
        prod = jnp.dot(lhs[:, :depth], rhs[:depth, :], preferred_element_type=F32)
        for r in range(ROWS):
            for j in range(2):
                out_ref[r, j] += prod[r * BLK:(r + 1) * BLK, j * BLK:(j + 1) * BLK]

    def loop(lo, hi, body):
        def step(i, carry):
            body(i)
            return carry
        lax.fori_loop(lo, hi, step, 0)

    @pl.when(core == 1)
    def _():
        own_part()
        t_copy(0, 0, sibling)
        z_step(1, 1)
        for n in range(2):
            done(piece, s_recv.at[0, 0, n])
            z_on(0, 0, 0, n)
            z_on(1, 0, 0, n)
        z_sent(1, 0)

        def ring(step):
            z_step(1, step)
            z_step(0, step - 1)

            @pl.when(step == 5)
            def _():
                done(tile, t_recv.at[7])
                tot[1] = part[7]
                for k in range(3):
                    t_copy(8 + k, 1, at_z(1 + k, 1))

            @pl.when(step == 6)
            def _():
                t_add(1, 2, (8, 9, 10))
                t_copy(11, 2, at_z(4, 1))
                t_copy(12, 2, at_z(-4, 1))

            z_sent(1, step - 1)
            s_sent(1, step - 1)
            z_sent(0, step - 2)

            @pl.when(step > 2)
            def _():
                s_sent(0, step - 2)

        loop(2, 7, ring)
        for n in range(2):
            done(piece, s_send.at[0, 1, n])
            for a in range(4):
                for b in range(4):
                    if a or b:
                        done(piece, q_recv.at[n, a, b])
        for copy in own_copies:
            copy.wait()

    @pl.when(core == 0)
    def _():
        def p_begin(who, n):
            src = zbuf.at[z, who, n]
            for way in (1, -1):
                p_first(src, who, n, 0, way)
                p_second(src, who, n, 0, 0, way)

        def take(who, n, a, b):
            done(piece, p_recv.at[who, n, p_at(a), p_at(b)])
            p_share(who, n, a, b)

        def first(a):
            def body(who, n):
                done(piece, p_recv.at[who, n, p_at(a), 0])
                src = p_ref(who, n, a, 0)
                if a == -1:
                    p_first(src, who, n, a, 1)
                p_second(src, who, n, a, 0, 1)
                p_second(src, who, n, a, 0, -1)
                p_share(who, n, a, 0)
            each(body)

        def second(a):
            def body(who, n):
                done(piece, p_recv.at[who, n, p_at(a), p_at(-1)])
                p_second(p_ref(who, n, a, -1), who, n, a, -1, 1)
                p_share(who, n, a, -1)
            each(body)

        for n in range(2):
            p_begin(0, n)
        own_part()
        for n in range(2):
            done(piece, s_recv.at[0, 1, n])
            p_begin(1, n)
        t_add(0, 1, (0,))
        for k in range(3):
            t_copy(1 + k, 1, at_xy(1 + k, 0, 0))
        t_add(1, 2, (1, 2, 3))
        for k in range(3):
            t_copy(4 + k, 2, at_xy(0, 1 + k, 0))
        first(-1)
        first(1)
        t_add(2, 3, (4, 5, 6))
        t_copy(7, 3, sibling)
        first(2)
        second(0)
        second(-1)
        second(1)
        second(2)
        for b in (1, 2):
            for a in (0, -1, 1, 2):
                each(lambda who, n, a=a, b=b: take(who, n, a, b))
        for copy in own_copies:
            copy.wait()
        for n in range(2):
            done(piece, s_send.at[0, 0, n])

        def sent(who, n):
            done(piece, p_send.at[who, n, 3, 0, 1])
            done(piece, p_send.at[who, n, 0, 0, 0])
            done(piece, p_send.at[who, n, 0, 0, 1])
            for a in range(4):
                done(piece, p_send.at[who, n, a, 0, 2])
                done(piece, p_send.at[who, n, a, 0, 3])
                done(piece, p_send.at[who, n, a, 3, 3])

            @pl.when(who == 1)
            def _():
                for a in range(4):
                    for b in range(4):
                        if a or b:
                            done(piece, q_send.at[n, a, b])
        each(sent)
        for k in (1, 2, 3, 4, 5, 6, 7):
            done(tile, t_send.at[k])

    def z_taken(i, count):
        @pl.when(core == 0)
        def _():
            for g in range(count):
                for n in range(2):
                    for who in range(2):
                        done(piece, s_recv.at[(spread(i + g) + NZ) % NZ, who, n])

    def four(i):
        @pl.when((core == 1) & (i == 2))
        def _():
            z_step(1, 7, last_hop)
            z_step(0, 6)
            done(tile, t_recv.at[11])
            send(part.at[11], part.at[13], t_send.at[13], t_recv.at[13], at_z(4, 1))

        @pl.when((core == 0) & (i == 0))
        def _():
            for g in range(1, 4):
                for n in range(2):
                    for who in range(2):
                        done(piece, s_recv.at[(spread(g) + NZ) % NZ, who, n])

        @pl.when(i > 0)
        def _():
            z_taken(4 * i, 4)

        compute(4 * i, 4)

    loop(0, 3, four)

    @pl.when(core == 1)
    def _():
        z_last(1)
        z_step(0, 7, last_hop)

    z_taken(12, 2)
    compute(12, 2)

    def one(i):
        @pl.when((core == 1) & (i == 14))
        def _():
            z_last(0)
            z_sent(1, 6)
            z_sent(0, 5)
            z_sent(0, 6)
            s_sent(1, 6)
            s_sent(0, 5)

        z_taken(i, 1)
        compute(i, 1)

    loop(14, 16, one)

    @pl.when(core == 1)
    def _():
        tail = tot[2] + part[11]
        for k in (12, 13):
            done(tile, t_recv.at[k])
            tail += part[k]
        tot[3] = tail
        t_copy(14, 3, sibling)
        tot[4] = tail
        for who in range(2):
            for n in range(2):
                done(piece, z_send.at[n, FAR - 1, who, n])
                done(piece, s_send.at[FAR, who, n])
            s_sent(who, 7)
        s_sent(0, 6)
        for k in (0, 8, 9, 10, 11, 12, 13, 14):
            done(tile, t_send.at[k])

    @pl.when(core == 0)
    def _():
        done(tile, t_recv.at[14])
        tot[4] = part[14]

    total = jnp.sum(jnp.sum(tot[4], axis=0, keepdims=True), axis=1, keepdims=True)
    occ_ref[...] = jnp.broadcast_to(total / (NX * NY * ROWS * BLK), occ_ref.shape)


def on_device(pattern, values, branch_sign):
    purified, occupation = pl.pallas_call(
        kernel,
        out_shape=(
            jax.ShapeDtypeStruct((ROWS, 2, BLK, BLK), F32),
            jax.ShapeDtypeStruct((8, BLK), F32),
        ),
        in_specs=[
            pl.BlockSpec(memory_space=pltpu.HBM),
            pl.BlockSpec(memory_space=pltpu.SMEM),
            pl.BlockSpec(memory_space=pltpu.HBM),
        ],
        out_specs=(
            pl.BlockSpec(memory_space=pltpu.VMEM),
            pl.BlockSpec(memory_space=pltpu.VMEM),
        ),
        scratch_shapes=[
            pltpu.VMEM((NZ, 2, 2, HALF, BLK), BF16),
            pltpu.VMEM((2, NX * NY, 2, HALF, BLK), BF16),
            pltpu.VMEM((ROWS * BLK, 4 * ROWS * BLK), BF16),
            pltpu.VMEM((4 * ROWS * BLK, PAIR), BF16),
            pltpu.VMEM((5, 8, BLK), F32),
            pltpu.VMEM((15, 8, BLK), F32),
            pltpu.SMEM((1, ROWS), jnp.int32),
            pltpu.SemaphoreType.DMA((2,)),
            pltpu.SemaphoreType.DMA((1,)),
            pltpu.SemaphoreType.DMA((2,)),
            pltpu.SemaphoreType.DMA((2, FAR, 2, 2)),
            pltpu.SemaphoreType.DMA((2, FAR + 1, 2, 2)),
            pltpu.SemaphoreType.DMA((NZ, 2, 2)),
            pltpu.SemaphoreType.DMA((NZ, 2, 2)),
            pltpu.SemaphoreType.DMA((2, 2, 4, 4, 4)),
            pltpu.SemaphoreType.DMA((2, 2, 4, 4)),
            pltpu.SemaphoreType.DMA((2, 4, 4)),
            pltpu.SemaphoreType.DMA((2, 4, 4)),
            pltpu.SemaphoreType.DMA((15,)),
            pltpu.SemaphoreType.DMA((15,)),
        ],
        compiler_params=pltpu.CompilerParams(
            collective_id=0, has_side_effects=True, vmem_limit_bytes=32 * 1024 * 1024),
        cost_estimate=pl.CostEstimate(flops=2 * 512 * 8192 * 256, bytes_accessed=1 << 20, transcendentals=0),
    )(pltpu.with_memory_space_constraint(pattern.reshape(1, ROWS), pltpu.HBM), branch_sign,
      pltpu.with_memory_space_constraint(values.reshape(ROWS * BLK, BLK), pltpu.HBM))
    return purified, occupation[0, 0]


def solution(mesh):
    in_specs = (P("row", "col"), P("row", "col", None, None), P())
    out_specs = (P("row", "col", None, None), P())
    return jax.shard_map(
        on_device, mesh=mesh, in_specs=in_specs, out_specs=out_specs, check_vma=False)
```

time: 55.6 us -> 52.9 us (0.951)
  local copies, waits for them, and re-layouts: 2.86 us -> 1.31 us
  Pallas kernels: 51.3 us -> 50.1 us
    unnamed x5 -> x1, local copies, waits for them, and re-layouts: 2.34 us -> 0.79 us
    pallas_call x1, Pallas kernels: 51.3 us -> 50.1 us  [on_device(): pl.pallas_call(kernel, out_shape=(jax.ShapeDtypeStruct((ROWS, 2, BLK, BLK...]
where the time goes in v3:
time: 52.9 us; the launch traced here: 52.7 us
  Pallas kernels  50.1 us (95%)
  local copies, waits for them, and re-layouts  1.31 us (2%)
  between operations  1.28 us (2%)
    pallas_call x1, Pallas kernels, on_device(): pl.pallas_call(kernel, out_shape=(jax.ShapeDtypeStruct((ROWS, 2, BLK, BLK...  50.1 us

profile of v3, /device:TPU:1, one launch (start us, length us, event | category | flops | bytes accessed | tf_op | source)
XLA Modules:
  0.0 52.7 jit_solution(17166124214747272339)
XLA Ops:
  1.3 50.1 %shard_map.50 = (f32[4,2,128,128]{3,2,1,0:T(8,128)S(1)}, f32[8,128]{1,0:T(8,128)S(1)}) custom-call(s32[1,4]{1,0:T(1,128)} %bitcast.4, s32[1]{0:T(128)S(6)} %copy.6.sign_ref, bf16[512,128]{1,0:T(8,128)(2,1)} %bitcast.3), custom_call_target="tpu_custom_call" | custom-call | flops 2147483648 | bytes 1048576 | tf_op jit(solution)/shard_map/pallas_call | solution.py:447
  51.4 0.5 slice.3
  51.9 0.8 %copy.7 = f32[4,2,128,128]{3,2,1,0:T(8,128)} copy(f32[4,2,128,128]{3,2,1,0:T(8,128)S(1)} %get-tuple-element.8) | data formatting | bytes 1048576

commit v4 on v3

--- a/solution.py
+++ b/solution.py
@@ -18,7 +18,7 @@
 
 def kernel(pat_hbm, sign_ref, val_ref, out_ref, occ_ref,
            zbuf, pbuf, lhs, rhs, tot, part, pat_ref, load_sem, small_sem, own_sem,
-           z_send, z_recv, s_send, s_recv, p_send, p_recv, q_send, q_recv, t_send, t_recv):
+           step_send, last_send, share_send, z_recv, s_recv, p_send, p_recv, q_send, q_recv, t_send, t_recv):
     row = lax.axis_index("row")
     col = lax.axis_index("col")
     y, x = row // NX, row % NX
@@ -91,8 +91,13 @@
     def done(ref, sem):
         pltpu.make_async_copy(ref, ref, sem).wait()
 
-    piece = zbuf.at[0, 0, 0]
-    tile = tot.at[0]
+    def taken(pieces, sem):
+        some = {1: zbuf.at[0, 0, 0], 2: zbuf.at[0, 0], 4: zbuf.at[0], 6: zbuf.at[pl.ds(0, 3), 0],
+                8: zbuf.at[pl.ds(0, 2)], 30: pbuf.at[0, pl.ds(0, 15)], 60: zbuf.at[pl.ds(0, 15)]}
+        done(some[pieces], sem)
+
+    def tiles(count, sem):
+        done(part.at[pl.ds(0, count)], sem)
 
     def z_ref(dz, who, n):
         return zbuf.at[slot_z(dz), who, n]
@@ -101,39 +106,28 @@
         return step * (2 * way - 1)
 
     def z_on(way, step, who, n):
-        dst = z_ref(z_shift(way, step), who, n)
-        send(dst, dst, z_send.at[way, step, who, n], z_recv.at[way, step + 1, who, n], at_z(1 - 2 * way, 1))
-
-    def z_share(dz, who, n):
-        dst = z_ref(dz, who, n)
-        k = (dz + NZ) % NZ
-        send(dst, dst, s_send.at[k, who, n], s_recv.at[k, who, n], sibling)
+        src = z_ref(z_shift(way, step), who, n)
+        send(src, src, step_send.at[who, step % 2], z_recv.at[way, step, who, n], at_z(1 - 2 * way, 1))
+
+    def z_share(dz, who, n, send_sem):
+        src = z_ref(dz, who, n)
+        send(src, src, send_sem, s_recv.at[(dz + NZ) % NZ], sibling)
 
     def z_step(who, step, on=lambda way, n: True):
         for n in range(2):
             for way in range(2):
-                done(piece, z_recv.at[way, step, who, n])
+                taken(1, z_recv.at[way, step - 1, who, n])
                 if on(way, n):
                     z_on(way, step, who, n)
-                z_share(z_shift(way, step), who, n)
+                z_share(z_shift(way, step), who, n, step_send.at[who, step % 2])
 
     def z_last(who):
         for n in range(2):
-            done(piece, z_recv.at[n, FAR, who, n])
-            z_share(FAR, who, n)
+            taken(1, z_recv.at[n, FAR - 1, who, n])
+            z_share(FAR, who, n, last_send)
 
     def last_hop(way, n):
         return way == n
-
-    def z_sent(who, step):
-        for n in range(2):
-            for way in range(2):
-                done(piece, z_send.at[way, step, who, n])
-
-    def s_sent(who, step):
-        for n in range(2):
-            done(piece, s_send.at[NZ - step, who, n])
-            done(piece, s_send.at[step, who, n])
 
     def p_xy(who, n, a, b):
         f = (1 - 2 * who) * (1 - 2 * n)
@@ -146,24 +140,25 @@
         return (a + 4) % 4
 
     def p_first(src, who, n, a, way):
-        send(src, p_ref(who, n, a, 0), p_send.at[who, n, p_at(a), 0, (way + 1) // 2],
-             p_recv.at[who, n, p_at(a - way), 0], at_xy(*p_xy(who, n, way, 0), 0))
+        send(src, p_ref(who, n, a, 0), p_send, p_recv.at[who, p_at(a - way), 0],
+             at_xy(*p_xy(who, n, way, 0), 0))
 
     def p_second(src, who, n, a, b, way):
-        send(src, p_ref(who, n, a, b), p_send.at[who, n, p_at(a), p_at(b), 2 + (way + 1) // 2],
-             p_recv.at[who, n, p_at(a), p_at(b - way)], at_xy(*p_xy(who, n, 0, way), 0))
-
-    def p_share(who, n, a, b):
+        send(src, p_ref(who, n, a, b), p_send, p_recv.at[who, p_at(a), p_at(b - way)],
+             at_xy(*p_xy(who, n, 0, way), 0))
+
+    def p_share(who, a, b):
         @pl.when(who == 1)
         def _():
-            src = p_ref(who, n, a, b)
-            send(src, src, q_send.at[n, p_at(a), p_at(b)], q_recv.at[n, p_at(a), p_at(b)], sibling)
+            for n in range(2):
+                src = p_ref(who, n, a, b)
+                send(src, src, q_send, q_recv, sibling)
 
     def each(body):
-        def step(i, carry):
-            body(i // 2, i % 2)
+        def step(who, carry):
+            body(who)
             return carry
-        lax.fori_loop(0, 4, step, 0)
+        lax.fori_loop(0, 2, step, 0)
 
     @pl.when(core == 1)
     def _():
@@ -172,7 +167,7 @@
             z_on(1, 0, 1, n)
 
     for n in range(2):
-        z_share(0, core, n)
+        z_share(0, core, n, share_send)
     own_copies = [
         pltpu.make_async_copy(zbuf.at[z, core, n], pbuf.at[core, row, n], own_sem.at[n]) for n in range(2)]
     for copy in own_copies:
@@ -194,13 +189,13 @@
             out_ref[i, 1] = twice * spots[i]
         tot[0] = sign * squares + (2.0 - 2.0 * odd) * diag
 
-    def t_copy(k, src, peer):
-        send(tot.at[src], part.at[k], t_send.at[k], t_recv.at[k], peer)
-
-    def t_add(src, dst, ks):
+    def t_copy(k, src, sem, peer):
+        send(tot.at[src], part.at[k], t_send, t_recv.at[sem], peer)
+
+    def t_add(src, dst, ks, sem):
         total = tot[src]
+        tiles(len(ks), t_recv.at[sem])
         for k in ks:
-            done(tile, t_recv.at[k])
             total += part[k]
         tot[dst] = total
 
@@ -241,13 +236,13 @@
     @pl.when(core == 1)
     def _():
         own_part()
-        t_copy(0, 0, sibling)
+        t_copy(0, 0, 0, sibling)
         z_step(1, 1)
-        for n in range(2):
-            done(piece, s_recv.at[0, 0, n])
+        taken(2, s_recv.at[0])
+        for n in range(2):
             z_on(0, 0, 0, n)
             z_on(1, 0, 0, n)
-        z_sent(1, 0)
+        taken(4, step_send.at[1, 0])
 
         def ring(step):
             z_step(1, step)
@@ -255,32 +250,30 @@
 
             @pl.when(step == 5)
             def _():
-                done(tile, t_recv.at[7])
+                tiles(1, t_recv.at[3])
                 tot[1] = part[7]
                 for k in range(3):
-                    t_copy(8 + k, 1, at_z(1 + k, 1))
+                    t_copy(8 + k, 1, 4, at_z(1 + k, 1))
 
             @pl.when(step == 6)
             def _():
-                t_add(1, 2, (8, 9, 10))
-                t_copy(11, 2, at_z(4, 1))
-                t_copy(12, 2, at_z(-4, 1))
-
-            z_sent(1, step - 1)
-            s_sent(1, step - 1)
-            z_sent(0, step - 2)
+                t_add(1, 2, (8, 9, 10), 4)
+                t_copy(11, 2, 5, at_z(4, 1))
+                t_copy(12, 2, 6, at_z(-4, 1))
+
+            taken(8, step_send.at[1, (step - 1) % 2])
+
+            @pl.when(step == 2)
+            def _():
+                taken(4, step_send.at[0, 0])
 
             @pl.when(step > 2)
             def _():
-                s_sent(0, step - 2)
+                taken(8, step_send.at[0, step % 2])
 
         loop(2, 7, ring)
-        for n in range(2):
-            done(piece, s_send.at[0, 1, n])
-            for a in range(4):
-                for b in range(4):
-                    if a or b:
-                        done(piece, q_recv.at[n, a, b])
+        taken(2, share_send)
+        taken(30, q_recv)
         for copy in own_copies:
             copy.wait()
 
@@ -292,44 +285,46 @@
                 p_first(src, who, n, 0, way)
                 p_second(src, who, n, 0, 0, way)
 
-        def take(who, n, a, b):
-            done(piece, p_recv.at[who, n, p_at(a), p_at(b)])
-            p_share(who, n, a, b)
+        def take(who, a, b):
+            taken(2, p_recv.at[who, p_at(a), p_at(b)])
+            p_share(who, a, b)
 
         def first(a):
-            def body(who, n):
-                done(piece, p_recv.at[who, n, p_at(a), 0])
-                src = p_ref(who, n, a, 0)
-                if a == -1:
-                    p_first(src, who, n, a, 1)
-                p_second(src, who, n, a, 0, 1)
-                p_second(src, who, n, a, 0, -1)
-                p_share(who, n, a, 0)
+            def body(who):
+                taken(2, p_recv.at[who, p_at(a), 0])
+                for n in range(2):
+                    src = p_ref(who, n, a, 0)
+                    if a == -1:
+                        p_first(src, who, n, a, 1)
+                    p_second(src, who, n, a, 0, 1)
+                    p_second(src, who, n, a, 0, -1)
+                p_share(who, a, 0)
             each(body)
 
         def second(a):
-            def body(who, n):
-                done(piece, p_recv.at[who, n, p_at(a), p_at(-1)])
-                p_second(p_ref(who, n, a, -1), who, n, a, -1, 1)
-                p_share(who, n, a, -1)
+            def body(who):
+                taken(2, p_recv.at[who, p_at(a), p_at(-1)])
+                for n in range(2):
+                    p_second(p_ref(who, n, a, -1), who, n, a, -1, 1)
+                p_share(who, a, -1)
             each(body)
 
         for n in range(2):
             p_begin(0, n)
         own_part()
-        for n in range(2):
-            done(piece, s_recv.at[0, 1, n])
+        taken(2, s_recv.at[0])
+        for n in range(2):
             p_begin(1, n)
-        t_add(0, 1, (0,))
+        t_add(0, 1, (0,), 0)
         for k in range(3):
-            t_copy(1 + k, 1, at_xy(1 + k, 0, 0))
-        t_add(1, 2, (1, 2, 3))
+            t_copy(1 + k, 1, 1, at_xy(1 + k, 0, 0))
+        t_add(1, 2, (1, 2, 3), 1)
         for k in range(3):
-            t_copy(4 + k, 2, at_xy(0, 1 + k, 0))
+            t_copy(4 + k, 2, 2, at_xy(0, 1 + k, 0))
         first(-1)
         first(1)
-        t_add(2, 3, (4, 5, 6))
-        t_copy(7, 3, sibling)
+        t_add(2, 3, (4, 5, 6), 2)
+        t_copy(7, 3, 3, sibling)
         first(2)
         second(0)
         second(-1)
@@ -337,53 +332,33 @@
         second(2)
         for b in (1, 2):
             for a in (0, -1, 1, 2):
-                each(lambda who, n, a=a, b=b: take(who, n, a, b))
+                each(lambda who, a=a, b=b: take(who, a, b))
         for copy in own_copies:
             copy.wait()
-        for n in range(2):
-            done(piece, s_send.at[0, 0, n])
-
-        def sent(who, n):
-            done(piece, p_send.at[who, n, 3, 0, 1])
-            done(piece, p_send.at[who, n, 0, 0, 0])
-            done(piece, p_send.at[who, n, 0, 0, 1])
-            for a in range(4):
-                done(piece, p_send.at[who, n, a, 0, 2])
-                done(piece, p_send.at[who, n, a, 0, 3])
-                done(piece, p_send.at[who, n, a, 3, 3])
-
-            @pl.when(who == 1)
-            def _():
-                for a in range(4):
-                    for b in range(4):
-                        if a or b:
-                            done(piece, q_send.at[n, a, b])
-        each(sent)
-        for k in (1, 2, 3, 4, 5, 6, 7):
-            done(tile, t_send.at[k])
+        taken(2, share_send)
+        taken(60, p_send)
+        taken(30, q_send)
+        tiles(7, t_send)
 
     def z_taken(i, count):
         @pl.when(core == 0)
         def _():
             for g in range(count):
-                for n in range(2):
-                    for who in range(2):
-                        done(piece, s_recv.at[(spread(i + g) + NZ) % NZ, who, n])
+                taken(4, s_recv.at[(spread(i + g) + NZ) % NZ])
 
     def four(i):
         @pl.when((core == 1) & (i == 2))
         def _():
             z_step(1, 7, last_hop)
             z_step(0, 6)
-            done(tile, t_recv.at[11])
-            send(part.at[11], part.at[13], t_send.at[13], t_recv.at[13], at_z(4, 1))
-
-        @pl.when((core == 0) & (i == 0))
-        def _():
-            for g in range(1, 4):
-                for n in range(2):
-                    for who in range(2):
-                        done(piece, s_recv.at[(spread(g) + NZ) % NZ, who, n])
+            tiles(1, t_recv.at[5])
+            send(part.at[11], part.at[13], t_send, t_recv.at[6], at_z(4, 1))
+            taken(8, step_send.at[1, 0])
+            taken(8, step_send.at[0, 1])
+
+        @pl.when(i == 0)
+        def _():
+            z_taken(1, 3)
 
         @pl.when(i > 0)
         def _():
@@ -405,11 +380,6 @@
         @pl.when((core == 1) & (i == 14))
         def _():
             z_last(0)
-            z_sent(1, 6)
-            z_sent(0, 5)
-            z_sent(0, 6)
-            s_sent(1, 6)
-            s_sent(0, 5)
 
         z_taken(i, 1)
         compute(i, 1)
@@ -419,24 +389,21 @@
     @pl.when(core == 1)
     def _():
         tail = tot[2] + part[11]
+        tiles(2, t_recv.at[6])
         for k in (12, 13):
-            done(tile, t_recv.at[k])
             tail += part[k]
         tot[3] = tail
-        t_copy(14, 3, sibling)
+        t_copy(14, 3, 7, sibling)
         tot[4] = tail
-        for who in range(2):
-            for n in range(2):
-                done(piece, z_send.at[n, FAR - 1, who, n])
-                done(piece, s_send.at[FAR, who, n])
-            s_sent(who, 7)
-        s_sent(0, 6)
-        for k in (0, 8, 9, 10, 11, 12, 13, 14):
-            done(tile, t_send.at[k])
+        taken(6, step_send.at[1, 1])
+        taken(8, step_send.at[0, 0])
+        taken(6, step_send.at[0, 1])
+        taken(4, last_send)
+        tiles(8, t_send)
 
     @pl.when(core == 0)
     def _():
-        done(tile, t_recv.at[14])
+        tiles(1, t_recv.at[7])
         tot[4] = part[14]
 
     total = jnp.sum(jnp.sum(tot[4], axis=0, keepdims=True), axis=1, keepdims=True)
@@ -470,16 +437,17 @@
             pltpu.SemaphoreType.DMA((2,)),
             pltpu.SemaphoreType.DMA((1,)),
             pltpu.SemaphoreType.DMA((2,)),
+            pltpu.SemaphoreType.DMA((2, 2)),
+            pltpu.SemaphoreType.DMA,
+            pltpu.SemaphoreType.DMA,
             pltpu.SemaphoreType.DMA((2, FAR, 2, 2)),
-            pltpu.SemaphoreType.DMA((2, FAR + 1, 2, 2)),
-            pltpu.SemaphoreType.DMA((NZ, 2, 2)),
-            pltpu.SemaphoreType.DMA((NZ, 2, 2)),
-            pltpu.SemaphoreType.DMA((2, 2, 4, 4, 4)),
-            pltpu.SemaphoreType.DMA((2, 2, 4, 4)),
+            pltpu.SemaphoreType.DMA((NZ,)),
+            pltpu.SemaphoreType.DMA,
             pltpu.SemaphoreType.DMA((2, 4, 4)),
-            pltpu.SemaphoreType.DMA((2, 4, 4)),
-            pltpu.SemaphoreType.DMA((15,)),
-            pltpu.SemaphoreType.DMA((15,)),
+            pltpu.SemaphoreType.DMA,
+            pltpu.SemaphoreType.DMA,
+            pltpu.SemaphoreType.DMA,
+            pltpu.SemaphoreType.DMA((8,)),
         ],
         compiler_params=pltpu.CompilerParams(
             collective_id=0, has_side_effects=True, vmem_limit_bytes=32 * 1024 * 1024),

time: 52.9 us -> 48 us (0.907)
  Pallas kernels: 50.1 us -> 45.2 us
    pallas_call x1, Pallas kernels: 50.1 us -> 45.2 us  [on_device(): pl.pallas_call(kernel, out_shape=(jax.ShapeDtypeStruct((ROWS, 2, BLK, BLK...]
where the time goes in v4:
time: 48 us; the launch traced here: 47.8 us
  Pallas kernels  45.2 us (94%)
  local copies, waits for them, and re-layouts  1.31 us (3%)
  between operations  1.28 us (3%)
    pallas_call x1, Pallas kernels, on_device(): pl.pallas_call(kernel, out_shape=(jax.ShapeDtypeStruct((ROWS, 2, BLK, BLK...  45.2 us

profile of v4, /device:TPU:1, one launch (start us, length us, event | category | flops | bytes accessed | tf_op | source)
XLA Modules:
  0.0 47.8 jit_solution(13928252063675858399)
XLA Ops:
  1.3 45.2 %shard_map.50 = (f32[4,2,128,128]{3,2,1,0:T(8,128)S(1)}, f32[8,128]{1,0:T(8,128)S(1)}) custom-call(s32[1,4]{1,0:T(1,128)} %bitcast.4, s32[1]{0:T(128)S(6)} %copy.6.sign_ref, bf16[512,128]{1,0:T(8,128)(2,1)} %bitcast.3), custom_call_target="tpu_custom_call" | custom-call | flops 2147483648 | bytes 1048576 | tf_op jit(solution)/shard_map/pallas_call | solution.py:414
  46.5 0.5 %slice.3 = f32[1,1]{1,0:T(1,128)} slice(f32[8,128]{1,0:T(8,128)S(1)} %get-tuple-element.5), slice={[0:1], [0:1]} | slice | bytes 8 | tf_op jit(solution)/shard_map/slice | solution.py:457
  47.0 0.8 %copy.7 = f32[4,2,128,128]{3,2,1,0:T(8,128)} copy(f32[4,2,128,128]{3,2,1,0:T(8,128)S(1)} %get-tuple-element.8) | data formatting | bytes 1048576

commit v5 on v4

--- a/solution.py
+++ b/solution.py
@@ -21,14 +21,14 @@
            step_send, last_send, share_send, z_recv, s_recv, p_send, p_recv, q_send, q_recv, t_send, t_recv):
     row = lax.axis_index("row")
     col = lax.axis_index("col")
-    y, x = row // NX, row % NX
-    z, core = col // 2, col % 2
+    y, x = lax.div(row, NX), lax.rem(row, NX)
+    z, core = lax.div(col, 2), lax.rem(col, 2)
 
     def slot_z(dz):
-        return (z + dz + NZ) % NZ
+        return lax.rem(z + dz + NZ, NZ)
 
     def slot_xy(dx, dy):
-        return ((y + dy + NY) % NY) * NX + (x + dx + NX) % NX
+        return lax.rem(y + dy + NY, NY) * NX + lax.rem(x + dx + NX, NX)
 
     def at_z(dz, who):
         return (row, slot_z(dz) * 2 + who)
@@ -148,17 +148,14 @@
              at_xy(*p_xy(who, n, 0, way), 0))
 
     def p_share(who, a, b):
-        @pl.when(who == 1)
-        def _():
+        if who == 1:
             for n in range(2):
                 src = p_ref(who, n, a, b)
                 send(src, src, q_send, q_recv, sibling)
 
     def each(body):
-        def step(who, carry):
+        for who in range(2):
             body(who)
-            return carry
-        lax.fori_loop(0, 2, step, 0)
 
     @pl.when(core == 1)
     def _():
@@ -272,10 +269,16 @@
                 taken(8, step_send.at[0, step % 2])
 
         loop(2, 7, ring)
+        z_step(1, 7, last_hop)
+        z_step(0, 6)
+        tiles(1, t_recv.at[5])
+        send(part.at[11], part.at[13], t_send, t_recv.at[6], at_z(4, 1))
         taken(2, share_send)
         taken(30, q_recv)
         for copy in own_copies:
             copy.wait()
+        taken(8, step_send.at[1, 0])
+        taken(8, step_send.at[0, 1])
 
     @pl.when(core == 0)
     def _():
@@ -318,15 +321,15 @@
         t_add(0, 1, (0,), 0)
         for k in range(3):
             t_copy(1 + k, 1, 1, at_xy(1 + k, 0, 0))
+        first(-1)
+        first(1)
         t_add(1, 2, (1, 2, 3), 1)
         for k in range(3):
             t_copy(4 + k, 2, 2, at_xy(0, 1 + k, 0))
-        first(-1)
-        first(1)
+        first(2)
+        second(0)
         t_add(2, 3, (4, 5, 6), 2)
         t_copy(7, 3, 3, sibling)
-        first(2)
-        second(0)
         second(-1)
         second(1)
         second(2)
@@ -349,12 +352,8 @@
     def four(i):
         @pl.when((core == 1) & (i == 2))
         def _():
-            z_step(1, 7, last_hop)
-            z_step(0, 6)
-            tiles(1, t_recv.at[5])
-            send(part.at[11], part.at[13], t_send, t_recv.at[6], at_z(4, 1))
-            taken(8, step_send.at[1, 0])
-            taken(8, step_send.at[0, 1])
+            z_last(1)
+            z_step(0, 7, last_hop)
 
         @pl.when(i == 0)
         def _():
@@ -368,18 +367,20 @@
 
     loop(0, 3, four)
 
-    @pl.when(core == 1)
-    def _():
-        z_last(1)
-        z_step(0, 7, last_hop)
-
     z_taken(12, 2)
     compute(12, 2)
 
     def one(i):
-        @pl.when((core == 1) & (i == 14))
+        @pl.when((core == 1) & (i == 15))
         def _():
             z_last(0)
+            tail = tot[2] + part[11]
+            tiles(2, t_recv.at[6])
+            for k in (12, 13):
+                tail += part[k]
+            tot[3] = tail
+            t_copy(14, 3, 7, sibling)
+            tot[4] = tail
 
         z_taken(i, 1)
         compute(i, 1)
@@ -388,13 +389,6 @@
 
     @pl.when(core == 1)
     def _():
-        tail = tot[2] + part[11]
-        tiles(2, t_recv.at[6])
-        for k in (12, 13):
-            tail += part[k]
-        tot[3] = tail
-        t_copy(14, 3, 7, sibling)
-        tot[4] = tail
         taken(6, step_send.at[1, 1])
         taken(8, step_send.at[0, 0])
         taken(6, step_send.at[0, 1])

time: 48 us -> 45.8 us (0.954)
  Pallas kernels: 45.2 us -> 43.1 us
    pallas_call x1, Pallas kernels: 45.2 us -> 43.1 us  [on_device(): pl.pallas_call(kernel, out_shape=(jax.ShapeDtypeStruct((ROWS, 2, BLK, BLK...]
where the time goes in v5:
time: 45.8 us; the launch traced here: 45.7 us
  Pallas kernels  43.1 us (94%)
  local copies, waits for them, and re-layouts  1.31 us (3%)
  between operations  1.28 us (3%)
    pallas_call x1, Pallas kernels, on_device(): pl.pallas_call(kernel, out_shape=(jax.ShapeDtypeStruct((ROWS, 2, BLK, BLK...  43.1 us

profile of v5, /device:TPU:1, one launch (start us, length us, event | category | flops | bytes accessed | tf_op | source)
XLA Modules:
  0.0 45.7 jit_solution(14679031654820605484)
XLA Ops:
  1.3 43.1 %shard_map.50 = (f32[4,2,128,128]{3,2,1,0:T(8,128)S(1)}, f32[8,128]{1,0:T(8,128)S(1)}) custom-call(s32[1,4]{1,0:T(1,128)} %bitcast.4, s32[1]{0:T(128)S(6)} %copy.6.sign_ref, bf16[512,128]{1,0:T(8,128)(2,1)} %bitcast.3), custom_call_target="tpu_custom_call" | custom-call | flops 2147483648 | bytes 1048576 | tf_op jit(solution)/shard_map/pallas_call | solution.py:408
  44.4 0.5 %slice.3 = f32[1,1]{1,0:T(1,128)} slice(f32[8,128]{1,0:T(8,128)S(1)} %get-tuple-element.5), slice={[0:1], [0:1]} | slice | bytes 8 | tf_op jit(solution)/shard_map/slice | solution.py:451
  44.9 0.8 %copy.7 = f32[4,2,128,128]{3,2,1,0:T(8,128)} copy(f32[4,2,128,128]{3,2,1,0:T(8,128)S(1)} %get-tuple-element.8) | data formatting | bytes 1048576

commit v6 on v5

--- a/solution.py
+++ b/solution.py
@@ -119,6 +119,7 @@
                 taken(1, z_recv.at[way, step - 1, who, n])
                 if on(way, n):
                     z_on(way, step, who, n)
+            for way in range(2):
                 z_share(z_shift(way, step), who, n, step_send.at[who, step % 2])
 
     def z_last(who):
@@ -245,14 +246,14 @@
             z_step(1, step)
             z_step(0, step - 1)
 
-            @pl.when(step == 5)
+            @pl.when(step == 4)
             def _():
                 tiles(1, t_recv.at[3])
                 tot[1] = part[7]
                 for k in range(3):
                     t_copy(8 + k, 1, 4, at_z(1 + k, 1))
 
-            @pl.when(step == 6)
+            @pl.when(step == 5)
             def _():
                 t_add(1, 2, (8, 9, 10), 4)
                 t_copy(11, 2, 5, at_z(4, 1))
@@ -270,9 +271,9 @@
 
         loop(2, 7, ring)
         z_step(1, 7, last_hop)
-        z_step(0, 6)
         tiles(1, t_recv.at[5])
         send(part.at[11], part.at[13], t_send, t_recv.at[6], at_z(4, 1))
+        z_step(0, 6)
         taken(2, share_send)
         taken(30, q_recv)
         for copy in own_copies:
@@ -367,25 +368,22 @@
 
     loop(0, 3, four)
 
-    z_taken(12, 2)
-    compute(12, 2)
-
-    def one(i):
-        @pl.when((core == 1) & (i == 15))
-        def _():
-            z_last(0)
-            tail = tot[2] + part[11]
-            tiles(2, t_recv.at[6])
-            for k in (12, 13):
-                tail += part[k]
-            tot[3] = tail
-            t_copy(14, 3, 7, sibling)
-            tot[4] = tail
-
-        z_taken(i, 1)
-        compute(i, 1)
-
-    loop(14, 16, one)
+    z_taken(12, 3)
+    compute(12, 3)
+
+    @pl.when(core == 1)
+    def _():
+        z_last(0)
+        tail = tot[2] + part[11]
+        tiles(2, t_recv.at[6])
+        for k in (12, 13):
+            tail += part[k]
+        tot[3] = tail
+        t_copy(14, 3, 7, sibling)
+        tot[4] = tail
+
+    z_taken(15, 1)
+    compute(15, 1)
 
     @pl.when(core == 1)
     def _():

time: 45.8 us -> 45.8 us (level)
  no operation moved by 1% of the time
where the time goes in v6:
time: 45.8 us; the launch traced here: 45.6 us
  Pallas kernels  43 us (94%)
  local copies, waits for them, and re-layouts  1.31 us (3%)
  between operations  1.28 us (3%)
    pallas_call x1, Pallas kernels, on_device(): pl.pallas_call(kernel, out_shape=(jax.ShapeDtypeStruct((ROWS, 2, BLK, BLK...  43 us

profile of v6, /device:TPU:1, one launch (start us, length us, event | category | flops | bytes accessed | tf_op | source)
XLA Modules:
  0.0 45.6 jit_solution(103163690937888649)
XLA Ops:
  1.3 43.0 %shard_map.50 = (f32[4,2,128,128]{3,2,1,0:T(8,128)S(1)}, f32[8,128]{1,0:T(8,128)S(1)}) custom-call(s32[1,4]{1,0:T(1,128)} %bitcast.4, s32[1]{0:T(128)S(6)} %copy.6.sign_ref, bf16[512,128]{1,0:T(8,128)(2,1)} %bitcast.3), custom_call_target="tpu_custom_call" | custom-call | flops 2147483648 | bytes 1048576 | tf_op jit(solution)/shard_map/pallas_call | solution.py:406
  44.3 0.5 %slice.3 = f32[1,1]{1,0:T(1,128)} slice(f32[8,128]{1,0:T(8,128)S(1)} %get-tuple-element.5), slice={[0:1], [0:1]} | slice | bytes 8 | tf_op jit(solution)/shard_map/slice | solution.py:449
  44.8 0.8 %copy.7 = f32[4,2,128,128]{3,2,1,0:T(8,128)} copy(f32[4,2,128,128]{3,2,1,0:T(8,128)S(1)} %get-tuple-element.8) | data formatting | bytes 1048576

commit v7 on v5

--- a/solution.py
+++ b/solution.py
@@ -93,7 +93,7 @@
 
     def taken(pieces, sem):
         some = {1: zbuf.at[0, 0, 0], 2: zbuf.at[0, 0], 4: zbuf.at[0], 6: zbuf.at[pl.ds(0, 3), 0],
-                8: zbuf.at[pl.ds(0, 2)], 30: pbuf.at[0, pl.ds(0, 15)], 60: zbuf.at[pl.ds(0, 15)]}
+                8: zbuf.at[pl.ds(0, 2)], 16: zbuf.at[pl.ds(0, 4)], 30: pbuf.at[0, pl.ds(0, 15)], 60: zbuf.at[pl.ds(0, 15)]}
         done(some[pieces], sem)
 
     def tiles(count, sem):
@@ -139,12 +139,20 @@
     def p_at(a):
         return (a + 4) % 4
 
+    def p_sem(who, a, b):
+        a, b = p_at(a), p_at(b)
+        if b == 0:
+            return 7 * who + a - 1
+        if b == 3:
+            return 7 * who + 3 + a
+        return 14 if who == 0 else 11 + 4 * b + a
+
     def p_first(src, who, n, a, way):
-        send(src, p_ref(who, n, a, 0), p_send, p_recv.at[who, p_at(a - way), 0],
+        send(src, p_ref(who, n, a, 0), p_send, p_recv.at[p_sem(who, a - way, 0)],
              at_xy(*p_xy(who, n, way, 0), 0))
 
     def p_second(src, who, n, a, b, way):
-        send(src, p_ref(who, n, a, b), p_send, p_recv.at[who, p_at(a), p_at(b - way)],
+        send(src, p_ref(who, n, a, b), p_send, p_recv.at[p_sem(who, a, b - way)],
              at_xy(*p_xy(who, n, 0, way), 0))
 
     def p_share(who, a, b):
@@ -289,12 +297,12 @@
                 p_second(src, who, n, 0, 0, way)
 
         def take(who, a, b):
-            taken(2, p_recv.at[who, p_at(a), p_at(b)])
+            taken(2, p_recv.at[p_sem(who, a, b)])
             p_share(who, a, b)
 
         def first(a):
             def body(who):
-                taken(2, p_recv.at[who, p_at(a), 0])
+                taken(2, p_recv.at[p_sem(who, a, 0)])
                 for n in range(2):
                     src = p_ref(who, n, a, 0)
                     if a == -1:
@@ -306,7 +314,7 @@
 
         def second(a):
             def body(who):
-                taken(2, p_recv.at[who, p_at(a), p_at(-1)])
+                taken(2, p_recv.at[p_sem(who, a, -1)])
                 for n in range(2):
                     p_second(p_ref(who, n, a, -1), who, n, a, -1, 1)
                 p_share(who, a, -1)
@@ -335,7 +343,8 @@
         second(2)
         for b in (1, 2):
             for a in (0, -1, 1, 2):
-                each(lambda who, a=a, b=b: take(who, a, b))
+                take(1, a, b)
+        taken(16, p_recv.at[p_sem(0, 0, 1)])
         for copy in own_copies:
             copy.wait()
         taken(2, share_send)
@@ -437,7 +446,7 @@
             pltpu.SemaphoreType.DMA((2, FAR, 2, 2)),
             pltpu.SemaphoreType.DMA((NZ,)),
             pltpu.SemaphoreType.DMA,
-            pltpu.SemaphoreType.DMA((2, 4, 4)),
+            pltpu.SemaphoreType.DMA((23,)),
             pltpu.SemaphoreType.DMA,
             pltpu.SemaphoreType.DMA,
             pltpu.SemaphoreType.DMA,

time: 45.8 us -> 45.8 us (level)
  no operation moved by 1% of the time
where the time goes in v7:
time: 45.8 us; the launch traced here: 45.6 us
  Pallas kernels  43 us (94%)
  local copies, waits for them, and re-layouts  1.31 us (3%)
  between operations  1.28 us (3%)
    pallas_call x1, Pallas kernels, on_device(): pl.pallas_call(kernel, out_shape=(jax.ShapeDtypeStruct((ROWS, 2, BLK, BLK...  43 us

profile of v7, /device:TPU:1, one launch (start us, length us, event | category | flops | bytes accessed | tf_op | source)
XLA Modules:
  0.0 45.6 jit_solution(7485660233339538739)
XLA Ops:
  1.3 43.0 %shard_map.50 = (f32[4,2,128,128]{3,2,1,0:T(8,128)S(1)}, f32[8,128]{1,0:T(8,128)S(1)}) custom-call(s32[1,4]{1,0:T(1,128)} %bitcast.4, s32[1]{0:T(128)S(6)} %copy.6.sign_ref, bf16[512,128]{1,0:T(8,128)(2,1)} %bitcast.3), custom_call_target="tpu_custom_call" | custom-call | flops 2147483648 | bytes 1048576 | tf_op jit(solution)/shard_map/pallas_call | solution.py:417
  44.3 0.5 %slice.3 = f32[1,1]{1,0:T(1,128)} slice(f32[8,128]{1,0:T(8,128)S(1)} %get-tuple-element.5), slice={[0:1], [0:1]} | slice | bytes 8 | tf_op jit(solution)/shard_map/slice | solution.py:460
  44.8 0.8 %copy.7 = f32[4,2,128,128]{3,2,1,0:T(8,128)} copy(f32[4,2,128,128]{3,2,1,0:T(8,128)S(1)} %get-tuple-element.8) | data formatting | bytes 1048576
